TPU v7x, 128 devices: a whole 4x4x4 slice. The times are simulated.
128 devices in a mesh: tm: 128 (over y, x, z, core).
Axes of the slice: x: 4, y: 4, z: 4, core: 2. Of those that a mesh axis runs over, the one named last changes fastest.
Arguments:
- filtered_mean: float32 [4096, 192], P('tm'), may hold values from -6 to 6
- filtered_cov: float32 [4096, 192, 192], P('tm'), may hold values from -0.2 to 1.35, as said below
- dynamics: float32 [4096, 192, 192], P('tm'), may hold values from -1 to 1
- predicted_precision: float32 [4096, 192, 192], P('tm'), may hold values from -1 to 2, as said below
Outputs:
- smoothed_state_means: float32 [4096, 192], P('tm')
- smooth_cov: float32 [4096, 192, 192], P('tm')
Inputs may be any that keep to these rules, and one draw needn't show every extreme that they name: `filtered_cov`: symmetric in its last two dimensions. `predicted_precision`: symmetric in its last two dimensions; for k >= 1, predicted_precision[k] is the inverse of a covariance that is at least dynamics[k-1] filtered_cov[k-1] dynamics[k-1]^T.
All inputs are finite; a program needn't handle non-finite values.
Results may differ from a plain program's by a relative error of at most 0.0003.
Values sent between devices are 32-bit elements; how exact they have to be, the bound alone decides.
No kernel may reach another device: no remote copies, remote signals or barrier semaphores. Data moves between devices by JAX's collectives and lax.ppermute only.
A program may use at most 192 MiB of HBM per device.

v0:
```python
import jax
import jax.numpy as jnp
from jax import lax
from jax.sharding import PartitionSpec as P

HIGH = lax.Precision.HIGHEST


def shifted(shard, axis, by):
    peers = lax.axis_size(axis)
    pairs = [(i, i + by) for i in range(peers) if 0 <= i + by < peers]
    return lax.ppermute(shard, axis, pairs)


def carried_in(shard, axis, combine, identity):
    peers, place = (lax.axis_size(axis), lax.axis_index(axis))
    everything = jax.tree.map(lambda part: lax.all_gather(part, axis), shard)
    start = jax.tree.map(
        lambda part, zero: jnp.broadcast_to(jnp.asarray(zero, part.dtype), part.shape),
        shard,
        identity,
    )

    def lap(k, before):
        at = peers - 1 - k
        reached = at > place
        new = combine(before, jax.tree.map(lambda part: part[at], everything))
        return jax.tree.map(lambda a, b: jnp.where(reached, a, b), new, before)

    return lax.fori_loop(0, peers, lap, start)


def compose(first, second):
    gain_one, offset_one, resid_one = first
    gain_two, offset_two, resid_two = second
    gain_new = jnp.matmul(gain_one, gain_two, precision=HIGH)
    offset_new = jnp.einsum("...ij,...j->...i", gain_one, offset_two, precision=HIGH) + offset_one
    gain_resid = jnp.matmul(gain_one, resid_two, precision=HIGH)
    resid_new = jnp.einsum("...ij,...mj->...im", gain_resid, gain_one, precision=HIGH) + resid_one
    return (gain_new, offset_new, resid_new)


def on_device(filtered_mean, filtered_cov, dynamics, predicted_precision):
    width = filtered_mean.shape[1]
    following = shifted(predicted_precision[:1], "tm", -1)
    precision_next = jnp.concatenate([predicted_precision[1:], following], 0)
    process_covariance = jnp.einsum("kij,klj->kil", filtered_cov, dynamics, precision=HIGH)
    gain_all = jnp.einsum("kij,kjl->kil", process_covariance, precision_next, precision=HIGH)
    predicted_state = jnp.einsum("kij,kj->ki", dynamics, filtered_mean, precision=HIGH)
    offset_all = filtered_mean - jnp.einsum("kij,kj->ki", gain_all, predicted_state, precision=HIGH)
    dyn_cov = jnp.einsum("kij,kjl->kil", dynamics, filtered_cov, precision=HIGH)
    resid_all = filtered_cov - jnp.einsum("kij,kjl->kil", gain_all, dyn_cov, precision=HIGH)
    scan_element_list = (gain_all, offset_all, resid_all)
    neutral_matrix = (
        jnp.eye(width, dtype=jnp.float32),
        jnp.zeros((width,), jnp.float32),
        jnp.zeros((width, width), jnp.float32),
    )

    def fold_only(carry, element):
        return (compose(element, carry), None)

    block = lax.scan(fold_only, neutral_matrix, scan_element_list, reverse=True)[0]

    def combine_parts(higher_part, lower_part):
        return compose(lower_part, higher_part)

    incoming = carried_in(block, "tm", combine_parts, neutral_matrix)
    offset_in = incoming[1]
    resid_in = incoming[2]

    def back_step(carry, element):
        mean_next, cov_next = carry
        gain, offset, resid = element
        mean_now = jnp.dot(gain, mean_next, precision=HIGH) + offset
        gain_cov = jnp.dot(gain, cov_next, precision=HIGH)
        cov_now = jnp.einsum("ij,mj->im", gain_cov, gain, precision=HIGH) + resid
        return ((mean_now, cov_now), (mean_now, cov_now))

    means, covs = lax.scan(back_step, (offset_in, resid_in), scan_element_list, reverse=True)[1]
    return (means, covs)


def solution(mesh):
    in_specs = (P("tm", None), P("tm", None, None), P("tm", None, None), P("tm", None, None))
    out_specs = (P("tm", None), P("tm", None, None))
    return jax.shard_map(
        on_device, mesh=mesh, in_specs=in_specs, out_specs=out_specs, check_vma=False
    )
```

profile of v0, /device:TPU:1, one launch (start us, length us, event | category | flops | bytes accessed | tf_op | source)
XLA Modules:
  0.0 1234.3 jit_solution(9515467761305441165)
XLA Ops:
  9.0 3.6 collective-permute-start
  12.6 14.1 %fusion.56 = f32[32,192,192]{2,1,0:T(8,128)} fusion(f32[32,192,192]{2,1,0:T(8,128)} %param.11, f32[32,192,192]{2,1,0:T(8,128)} %param.12), kind=kOutput, calls=%fused_computation.70 | convolution fusion | flops 2717908992 | bytes 14155776 | tf_op jit(solution)/shard_map/kij,klj->kil/dot_general | solution.py:47
  26.8 8.1 fusion.57
  34.9 5.5 fusion.53
  40.4 3.2 slice.6
  43.6 11.9 fusion.46
  55.6 12.3 convolution_subtract_fusion
  67.9 5.5 fusion.51
  73.4 165.9 %while.58 = (s32[]{:T(128)}, f32[192,192]{1,0:T(8,128)S(1)}, f32[192]{0:T(256)S(1)}, f32[192,192]{1,0:T(8,128)S(1)}, f32[32,192,192]{2,1,0:T(8,128)}, /*index=5*...) while((s32[]{:T(128)}, f32[192,192]{1,0:T(8,128)S(1)}, ...), condition=%wide.region_1.2_spmd.clone, body=%wide.region_0.1_spmd.clone.sunk | while | flops 255320448 | bytes 2170764 | solution.py:63
  241.8 139.2 %all-reduce.3.cloned.1.call-done = f32[24576]{0:T(1024)} async-done(((f32[24576]{0:T(1024)}), f32[24576]{0:T(1024)}) %all-reduce.3.cloned.1.call-update) | async-done | bytes 98320
  381.9 93.7 %all-gather.6.cloned.1.call-done = f32[24576,192]{1,0:T(8,128)} async-done(((f32[192,192]{1,0:T(8,128)}), f32[24576,192]{1,0:T(8,128)}) %all-gather.6.cloned.1.call-update) | async-done | bytes 18874384 | tf_op jit(solution)/shard_map/all_gather | solution.py:17
  475.6 96.0 %all-gather.8.cloned.1.call-done = f32[24576,192]{1,0:T(8,128)} async-done(((f32[192,192]{1,0:T(8,128)}), f32[24576,192]{1,0:T(8,128)}) %all-gather.8.cloned.1.call-update) | async-done | bytes 18874384 | tf_op jit(solution)/shard_map/all_gather | solution.py:17
  571.6 505.3 %while.59 = (s32[]{:T(128)}, f32[192]{0:T(256)S(1)}, f32[192,192]{1,0:T(8,128)S(1)}, s32[]{:T(128)}, f32[128,192,192]{2,1,0:T(8,128)}, /*index=5*/f32[128,192]{1...) while((s32[]{:T(128)}, f32[192]{0:T(256)S(1)}, ...), condition=%wide.region_3.4_spmd.clone, body=%wide.region_2.3_spmd.clone.sunk | while | flops 170459904 | bytes 1533629 | solution.py:30
  1076.9 3.4 broadcast_in_dim.35
  1080.3 146.9 %while.57 = (s32[]{:T(128)}, f32[192]{0:T(256)S(1)}, f32[192,192]{1,0:T(8,128)S(1)}, f32[32,192]{1,0:T(8,128)S(1)}, f32[32,192,192]{2,1,0:T(8,128)}, /*index=5*/...) while((s32[]{:T(128)}, f32[192]{0:T(256)S(1)}, ...), condition=%wide.region_5.6_spmd, body=%wide.region_4.5_spmd.sunk | while | flops 170348736 | bytes 1580937 | solution.py:80
  1082.9 2.1 bitcast_dynamic-update-slice_fusion.2
  1087.5 2.1 bitcast_dynamic-update-slice_fusion.2
  1092.0 2.1 bitcast_dynamic-update-slice_fusion.2
  1096.6 2.1 bitcast_dynamic-update-slice_fusion.2
  1101.2 2.1 bitcast_dynamic-update-slice_fusion.2
  1115.0 2.1 bitcast_dynamic-update-slice_fusion.2
  1174.7 2.1 bitcast_dynamic-update-slice_fusion.2
  1188.4 2.1 bitcast_dynamic-update-slice_fusion.2
  1202.2 2.1 bitcast_dynamic-update-slice_fusion.2
  (1258 shorter events, 793.8 us)
Async XLA Ops:
  7.2 373.8 %all-reduce.3.cloned.1.call-start = ((), (), s32[]{:S(2)}) async-start(), calls=%async_computation.2 | async-start | bytes 196608
  7.2 19.5 %slice-start = ((s8[6291456]{0:T(1024)(128)(4,1)}), s8[4194304]{0:T(1024)(128)(4,1)S(1)}, s32[]{:S(2)}) async-start(s8[6291456]{0:T(1024)(128)(4,1)} %bitcast.131), calls=%async_computation.3 | async-start | bytes 8388608
  7.2 19.5 %slice-start.2 = ((s8[6291456]{0:T(1024)(128)(4,1)}), s8[4194304]{0:T(1024)(128)(4,1)S(1)}, s32[]{:S(2)}) async-start(s8[6291456]{0:T(1024)(128)(4,1)} %bitcast.133), calls=%async_computation.5 | async-start | bytes 8388608
  9.0 17.7 %slice-start.1 = ((s8[6291456]{0:T(1024)(128)(4,1)}), s8[2097152]{0:T(1024)(128)(4,1)S(1)}, s32[]{:S(2)}) async-start(s8[6291456]{0:T(1024)(128)(4,1)} %bitcast.131), calls=%async_computation.4 | async-start | bytes 4194304
  9.0 17.7 %slice-start.3 = ((s8[6291456]{0:T(1024)(128)(4,1)}), s8[2097152]{0:T(1024)(128)(4,1)S(1)}, s32[]{:S(2)}) async-start(s8[6291456]{0:T(1024)(128)(4,1)} %bitcast.133), calls=%async_computation.6 | async-start | bytes 4194304
  9.0 34.6 %collective-permute-start = (f32[1,192,192]{2,1,0:T(8,128)}, f32[1,192,192]{2,1,0:T(8,128)}, u32[]{:S(2)}, u32[]{:S(2)}) collective-permute-start(f32[1,192,192]{2,1,0:T(8,128)} %slice.7), channel_id=1, source_target_pairs={{1,0},{2,1},{3,2},{4,3},{5,4},{6,5},{7,6},{8,7},{9,8},{10,9},{11,1... | collective-permute-start | bytes 442376 | tf_op jit(solution)/shard_map/ppermute | solution.py:12
  12.6 27.8 %slice-start.6 = ((s8[6291456]{0:T(1024)(128)(4,1)}), s8[4194304]{0:T(1024)(128)(4,1)S(1)}, s32[]{:S(2)}) async-start(s8[6291456]{0:T(1024)(128)(4,1)} %bitcast.137), calls=%async_computation.9 | async-start | bytes 8388608
  26.7 8.2 copy-start.4
  26.7 13.6 %slice-start.7 = ((s8[6291456]{0:T(1024)(128)(4,1)}), s8[2097152]{0:T(1024)(128)(4,1)S(1)}, s32[]{:S(2)}) async-start(s8[6291456]{0:T(1024)(128)(4,1)} %bitcast.137), calls=%async_computation.10 | async-start | bytes 4194304
  43.6 11.9 slice-start.4
  43.6 11.9 slice-start.5
  55.5 12.3 copy-start
  239.3 1.0 copy-start.1
  239.3 1.8 copy-start.2
  239.6 0.6 copy-start.3
  240.2 235.4 %all-gather.6.cloned.1.call-start = ((), (), s32[]{:S(2)}) async-start(), calls=%async_computation | async-start | bytes 25362432 | tf_op jit(solution)/shard_map/all_gather | solution.py:17
  241.0 330.6 %all-gather.8.cloned.1.call-start = ((), (), s32[]{:S(2)}) async-start(), calls=%async_computation.1 | async-start | bytes 25362432 | tf_op jit(solution)/shard_map/all_gather | solution.py:17
  1227.2 0.6 copy-start.5
Sparse Core Ops, SparseCore 0:
  240.4 140.4 all-reduce.2
  384.9 90.6 all-gather.5
  479.1 92.4 all-gather.7
where the time goes:
time: 1250 us; the launch traced here: 1230 us
  matrix products  846 us (68%)
  waiting for transfers between devices  330 us (26%)
  local copies, waits for them, and re-layouts  25.5 us (2%)
  between operations  14 us (1%)
    dot_general x160, matrix products, compose(): jnp.einsum('...ij,...mj->...im', gain_resid, gain_one, precision=HIGH)  223 us
    dot_general x160, matrix products, compose(): gain_resid = jnp.matmul(gain_one, resid_two, precision=HIGH)  200 us
    all_gather x2, waiting for transfers between devices, carried_in(): everything = jax.tree.map(lambda part: lax.all_gather(part, axis), shard)  190 us
    dot_general x160, matrix products, compose(): jnp.einsum('...ij,...j->...i', gain_one, offset_two, precision=HIGH)  184 us
    unnamed x4, waiting for transfers between devices  141 us
    dot_general x32, matrix products, back_step(): cov_now = jnp.einsum('ij,mj->im', gain_cov, gain, precision=HIGH) + resid  65.8 us
    dot_general x32, matrix products, back_step(): gain_cov = jnp.dot(gain, cov_next, precision=HIGH)  40 us
    dot_general x32, matrix products, compose(): gain_new = jnp.matmul(gain_one, gain_two, precision=HIGH)  39.9 us
  transfers between devices with their start and end apart: 4, of which 3 were waited for; matrix products, arithmetic and copies ran while one was open for 3% of the time, Pallas kernels for 0%

commit v1 on v0

v1 whole, which is shorter than its diff:
```python
import jax
import jax.numpy as jnp
from jax import lax
from jax.experimental import pallas as pl
from jax.experimental.pallas import tpu as pltpu
from jax.sharding import PartitionSpec as P

HIGHEST = lax.Precision.HIGHEST
F32 = jnp.float32
W = 192
STEPS = 8
ROWS = 592
HALF = ROWS // 2
VMEM_LIMIT = 60 << 20


def times(a, b):
    return jnp.dot(a, b, precision=HIGHEST, preferred_element_type=F32)


def times_t(a, b):
    return lax.dot_general(
        a, b, (((1,), (1,)), ((), ())), precision=HIGHEST, preferred_element_type=F32
    )


def split(x):
    high = x.astype(jnp.bfloat16)
    return high, (x - high.astype(F32)).astype(jnp.bfloat16)


def three(a, b, side):
    def part(x, y):
        return lax.dot_general(x, y, (((1,), (side,)), ((), ())), preferred_element_type=F32)

    return part(a[0], b[0]) + (part(a[0], b[1]) + part(a[1], b[0]))


def packed(e, l, u, ref):
    ref[0:192, :] = e[:, :128]
    ref[192:384, :] = jnp.concatenate([e[:, 128:], l[:, 128:]], 1)
    ref[384:576, :] = l[:, :128]
    ref[576:592, :] = jnp.zeros((16, 128), F32)
    ref[576:577, :] = u[0:1, :128]
    ref[577:578, 0:64] = u[0:1, 128:]


def unpacked(ref):
    tail = ref[192:384, :]
    e = jnp.concatenate([ref[0:192, :], tail[:, :64]], 1)
    l = jnp.concatenate([ref[384:576, :], tail[:, 64:]], 1)
    u = jnp.concatenate([ref[576:577, :], ref[577:578, 0:64]], 1)
    return e, l, jnp.broadcast_to(u, (16, W))


def applied(e, l, u, cov, mean):
    left = three(e, cov, 0)
    both = three(split(jnp.concatenate([left, mean], 0)), e, 1)
    return both[:W] + l, both[W:] + u


def composed(first, second):
    e = split(first[0])
    l, u = applied(e, first[1], first[2], split(second[1]), second[2])
    return three(e, split(second[0]), 0), l, u


def in_three(rows):
    high = rows.astype(jnp.bfloat16).astype(F32)
    rest = rows - high
    middle = rest.astype(jnp.bfloat16).astype(F32)
    at = lax.broadcasted_iota(jnp.int32, (16, W), 0)
    tail = jnp.where(at == 2, rest - middle, 0.0)
    return jnp.where(at == 0, high, jnp.where(at == 1, middle, tail))


def eye():
    return (
        lax.broadcasted_iota(jnp.int32, (W, W), 0) == lax.broadcasted_iota(jnp.int32, (W, W), 1)
    ).astype(F32)


def cross_kernel(mean, cov, dyn, cross, moved):
    for j in range(STEPS):
        rows = jnp.concatenate([cov[j], jnp.broadcast_to(mean[j : j + 1], (8, W))], 0)
        both = times_t(rows, dyn[j])
        cross[j] = both[:W]
        moved[j : j + 1] = both[W : W + 1]


def fold_kernel(
    following, mean, cov, cross, moved, precision, e_out, l_out, u_out, total, nxt, e_now, l_now, u_now
):
    @pl.when(pl.program_id(0) == 0)
    def _():
        nxt[...] = following[0]
        e_now[...] = eye()
        l_now[...] = jnp.zeros((W, W), F32)
        u_now[...] = jnp.zeros((16, W), F32)

    def element(j):
        after = nxt[...] if j == STEPS - 1 else precision[j + 1]
        gain = times(cross[j], after)
        return gain, cov[j] - times_t(gain, cross[j])

    e, l, u = e_now[...], l_now[...], u_now[...]
    ready = element(STEPS - 1)
    for j in reversed(range(STEPS)):
        gain, resid = ready
        if j:
            ready = element(j - 1)
        gain_split = split(gain)
        left = three(gain_split, split(l), 0)
        e = times(gain, e)
        rows = jnp.concatenate([left, in_three(u - moved[j : j + 1])], 0)
        both = three(split(rows), gain_split, 1)
        l = both[:W] + resid
        u = jnp.broadcast_to(jnp.sum(both[W:], 0, keepdims=True) + mean[j : j + 1], (16, W))
        e_out[j] = e
        l_out[j] = l
        u_out[j : j + 1] = u[0:1]
    nxt[...] = precision[0]
    e_now[...] = e
    l_now[...] = l
    u_now[...] = u

    @pl.when(pl.program_id(0) == pl.num_programs(0) - 1)
    def _():
        packed(e_now[...], l_now[...], u_now[...], total)


def pair_kernel(place, own, other, total, half, after):
    low = place[1] == 0

    @pl.when(low)
    def _():
        after[...] = other[...]
        packed(*composed(unpacked(own), unpacked(other)), total)

    @pl.when(jnp.logical_not(low))
    def _():
        packed(eye(), jnp.zeros((W, W), F32), jnp.zeros((16, W), F32), after)
        packed(*composed(unpacked(other), unpacked(own)), total)

    half[...] = total[pl.ds(pl.multiple_of(place[1] * HALF, 8), HALF), :]


def arrange(place, own, halves, ordered):
    spot, core = place[0], place[1]
    ordered[spot] = own[...]
    mine = pl.multiple_of(core * HALF, 8)
    theirs = pl.multiple_of((1 - core) * HALF, 8)
    for k in range(3):
        slot = lax.rem(spot + k + 1, 4)
        ordered[slot, pl.ds(mine, HALF), :] = halves[2 * k][...]
        ordered[slot, pl.ds(theirs, HALF), :] = halves[2 * k + 1][...]


def quad_kernel(place, own, *refs):
    halves, (total, half, ordered) = refs[:6], refs[6:]
    arrange(place, own, halves, ordered)
    parts = [unpacked(ordered.at[k]) for k in range(4)]
    early, late = composed(parts[0], parts[1]), composed(parts[2], parts[3])
    packed(*composed(early, late), total)
    half[...] = total[pl.ds(pl.multiple_of(place[1] * HALF, 8), HALF), :]


def join_kernel(place, near, own, *refs):
    halves, (joined, ordered) = refs[:6], refs[6:]
    arrange(place, own, halves, ordered)
    joined[...] = near[...]
    for k in (1, 2, 3):

        @pl.when(k > place[0])
        def _():
            packed(*composed(unpacked(joined), unpacked(ordered.at[k])), joined)


def advance(element, cov, mean):
    e, l, u = unpacked(element)
    cov[...], mean[...] = applied(split(e), l, u, split(cov[...]), mean[...])


def finish_kernel(place, near, own, *refs):
    halves, (e_all, l_all, u_all, mean_out, cov_out, ordered, cov_in, mean_in) = refs[:6], refs[6:]

    @pl.when(pl.program_id(0) == 0)
    def _():
        arrange(place, own, halves, ordered)
        cov_in[...] = jnp.zeros((W, W), F32)
        mean_in[...] = jnp.zeros((16, W), F32)
        for k in (3, 2, 1):

            @pl.when(k > place[0])
            def _():
                advance(ordered.at[k], cov_in, mean_in)

        advance(near, cov_in, mean_in)

    cov, mean = split(cov_in[...]), mean_in[...]
    for j in range(STEPS):
        now, u = applied(split(e_all[j]), l_all[j], u_all[j : j + 1], cov, mean)
        cov_out[j] = now
        mean_out[j : j + 1] = u[0:1]


def struct(*shape):
    return jax.ShapeDtypeStruct(shape, F32)


def cost(products, passes, size):
    return pl.CostEstimate(
        flops=products * passes * 2 * W**3, bytes_accessed=size, transcendentals=0
    )


PARAMS = pltpu.CompilerParams(vmem_limit_bytes=VMEM_LIMIT)
WHOLE = pl.BlockSpec(memory_space=pltpu.VMEM)
SCALAR = pl.BlockSpec(memory_space=pltpu.SMEM)
ELEMENT = ROWS * 128 * 4


def on_device(filtered_mean, filtered_cov, dynamics, predicted_precision):
    peers = lax.axis_size("tm")
    here = lax.axis_index("tm")
    count = filtered_mean.shape[0]
    blocks = count // STEPS
    matrices = count * W * 256 * 4

    following = lax.ppermute(
        predicted_precision[:1], "tm", [(i, i - 1) for i in range(1, peers)]
    )

    up = lambda i: (i, 0)
    up3 = lambda i: (i, 0, 0)
    vec, mat = pl.BlockSpec((STEPS, W), up), pl.BlockSpec((STEPS, W, W), up3)
    cross, moved = pl.pallas_call(
        cross_kernel,
        grid=(blocks,),
        in_specs=[vec, mat, mat],
        out_specs=[mat, vec],
        out_shape=[struct(count, W, W), struct(count, W)],
        compiler_params=PARAMS,
        cost_estimate=cost(count, 6, 3 * matrices),
        name="cross",
    )(filtered_mean, filtered_cov, dynamics)

    down = pl.BlockSpec((STEPS, W), lambda i: (blocks - 1 - i, 0))
    down3 = pl.BlockSpec((STEPS, W, W), lambda i: (blocks - 1 - i, 0, 0))
    once = pl.BlockSpec((1, W, W), lambda i: (0, 0, 0))
    e_all, l_all, u_all, total = pl.pallas_call(
        fold_kernel,
        grid=(blocks,),
        in_specs=[once, down, down3, down3, down, down3],
        out_specs=[down3, down3, down, pl.BlockSpec((ROWS, 128), lambda i: (0, 0))],
        out_shape=[struct(count, W, W), struct(count, W, W), struct(count, W), struct(ROWS, 128)],
        scratch_shapes=[
            pltpu.VMEM((W, W), F32),
            pltpu.VMEM((W, W), F32),
            pltpu.VMEM((W, W), F32),
            pltpu.VMEM((16, W), F32),
        ],
        compiler_params=PARAMS,
        cost_estimate=cost(5 * count, 6, 5 * matrices),
        name="fold",
    )(following, filtered_mean, filtered_cov, cross, moved, predicted_precision)

    def place(stride):
        return jnp.stack([lax.rem(lax.div(here, stride), 4), lax.rem(here, 2)])

    def other_core(part):
        return lax.ppermute(part, "tm", [(i, i ^ 1) for i in range(peers)])

    total, half, near = pl.pallas_call(
        pair_kernel,
        in_specs=[SCALAR, WHOLE, WHOLE],
        out_specs=[WHOLE] * 3,
        out_shape=[struct(ROWS, 128), struct(HALF, 128), struct(ROWS, 128)],
        compiler_params=PARAMS,
        cost_estimate=cost(3, 3, 4 * ELEMENT),
        name="pair",
    )(place(1), total, other_core(total))

    def gathered(half, stride, later_only):
        got = [None] * 3
        for k in (2, 1, 3):
            pairs = []
            for i in range(peers):
                spot = i // stride % 4
                if spot + k < 4 or not later_only:
                    pairs.append((i + ((spot + k) % 4 - spot) * stride, i))
            mine = lax.ppermute(half, "tm", pairs)
            got[k - 1] = (mine, other_core(mine))
        return [part for two in got for part in two]

    for stride in (2, 8):
        parts = gathered(half, stride, False)
        own = total
        total, half = pl.pallas_call(
            quad_kernel,
            in_specs=[SCALAR] + [WHOLE] * 7,
            out_specs=[WHOLE, WHOLE],
            out_shape=[struct(ROWS, 128), struct(HALF, 128)],
            scratch_shapes=[pltpu.VMEM((4, ROWS, 128), F32)],
            compiler_params=PARAMS,
            cost_estimate=cost(9, 3, 6 * ELEMENT),
            name="quad",
        )(place(stride), own, *parts)
        near = pl.pallas_call(
            join_kernel,
            in_specs=[SCALAR] + [WHOLE] * 8,
            out_specs=WHOLE,
            out_shape=struct(ROWS, 128),
            scratch_shapes=[pltpu.VMEM((4, ROWS, 128), F32)],
            compiler_params=PARAMS,
            cost_estimate=cost(9, 3, 6 * ELEMENT),
            name="join",
        )(place(stride), near, own, *parts)

    parts = gathered(half, 32, True)
    flat = pl.BlockSpec((ROWS, 128), lambda i: (0, 0))
    flat_half = pl.BlockSpec((HALF, 128), lambda i: (0, 0))
    return pl.pallas_call(
        finish_kernel,
        grid=(blocks,),
        in_specs=[SCALAR] + [flat] * 2 + [flat_half] * 6 + [mat, mat, vec],
        out_specs=[vec, mat],
        out_shape=[struct(count, W), struct(count, W, W)],
        scratch_shapes=[
            pltpu.VMEM((4, ROWS, 128), F32),
            pltpu.VMEM((W, W), F32),
            pltpu.VMEM((16, W), F32),
        ],
        compiler_params=PARAMS,
        cost_estimate=cost(2 * count, 3, 3 * matrices),
        name="finish",
    )(place(32), near, total, *parts, e_all, l_all, u_all)


def solution(mesh):
    in_specs = (P("tm", None), P("tm", None, None), P("tm", None, None), P("tm", None, None))
    out_specs = (P("tm", None), P("tm", None, None))
    return jax.shard_map(
        lambda *args: tuple(on_device(*args)),
        mesh=mesh,
        in_specs=in_specs,
        out_specs=out_specs,
        check_vma=False,
    )
```

time: 1250 us -> 133 us (0.11); the launches traced: 1230 us -> 132 us
  matrix products: 846 us -> 0 us
  waiting for transfers between devices: 330 us -> 22.8 us
  Pallas kernels: 0 us -> 77.5 us
  local copies, waits for them, and re-layouts: 25.5 us -> 4.35 us
  starting transfers between devices: 3.7 us -> 24.3 us
  between operations: 14 us -> 0.81 us
    dot_general x614 -> x0, matrix products: 846 us -> none  [the longest x160 223 us: compose(): jnp.einsum('...ij,...mj->...im', gain_resid, gain_one, precision=HIGH)]
    all_gather x2 -> x0, waiting for transfers between devices: 190 us -> none  [carried_in(): everything = jax.tree.map(lambda part: lax.all_gather(part, axis), shard)]
    unnamed x4 -> x0, waiting for transfers between devices: 141 us -> none
    pallas_call x0 -> x8, Pallas kernels: none -> 77.5 us  [the longest x1 34.5 us: on_device(): pl.pallas_call(fold_kernel, grid=(blocks,), in_specs=[once, down, down3,...]
    ppermute x1 -> x20, waiting for transfers between devices: 0.01 us -> 22.8 us  [the longest x9 20.4 us: gathered(): mine = lax.ppermute(half, 'tm', pairs)]
    ppermute x1 -> x20, starting transfers between devices: 3.58 us -> 24.3 us  [the longest x9 15.5 us: gathered(): mine = lax.ppermute(half, 'tm', pairs)]
    dynamic_slice x192 -> x0, local copies, waits for them, and re-layouts: 12.6 us -> none  [the longest x128 8.42 us: lap(): new = combine(before, jax.tree.map(lambda part: part[at], everything))]
  transfers between devices with their start and end apart: 4 -> 20, of which waited for: 3 -> 10; matrix products, arithmetic and copies ran while one was open for 3% -> 2% of each run, Pallas kernels for 0% -> 14%
where the time goes in v1:
time: 133 us; the launch traced here: 132 us
  Pallas kernels  77.5 us (58%)
  starting transfers between devices  24.3 us (18%)
  waiting for transfers between devices  22.8 us (17%)
  local copies, waits for them, and re-layouts  4.35 us (3%)
  other arithmetic  2.44 us (2%)
    pallas_call x1, Pallas kernels, on_device(): pl.pallas_call(fold_kernel, grid=(blocks,), in_specs=[once, down, down3,...  34.5 us
    ppermute x9, waiting for transfers between devices, gathered(): mine = lax.ppermute(half, 'tm', pairs)  20.4 us
    ppermute x9, starting transfers between devices, gathered(): mine = lax.ppermute(half, 'tm', pairs)  15.5 us
    pallas_call x1, Pallas kernels, on_device(): pl.pallas_call(finish_kernel, grid=(blocks,), in_specs=[SCALAR] + [flat]...  14.2 us
    pallas_call x1, Pallas kernels, on_device(): pl.pallas_call(cross_kernel, grid=(blocks,), in_specs=[vec, mat, mat], ou...  10.6 us
    pallas_call x2, Pallas kernels, on_device(): pl.pallas_call(join_kernel, in_specs=[SCALAR] + [WHOLE] * 8, out_specs=WH...  8.24 us
    pallas_call x2, Pallas kernels, on_device(): pl.pallas_call(quad_kernel, in_specs=[SCALAR] + [WHOLE] * 7, out_specs=[W...  7.42 us
    ppermute x10, starting transfers between devices, other_core(): return lax.ppermute(part, 'tm', [(i, i ^ 1) for i in range(peers)])  5.49 us
  transfers between devices with their start and end apart: 20, of which 10 were waited for; matrix products, arithmetic and copies ran while one was open for 2% of the time, Pallas kernels for 14%

profile of v1, /device:TPU:1, one launch (start us, length us, event | category | flops | bytes accessed | tf_op | source)
XLA Modules:
  0.0 132.2 jit_solution(13124268758406083363)
XLA Ops:
  1.6 3.3 %collective-permute-start = (f32[1,192,192]{2,1,0:T(8,128)S(1)}, f32[1,192,192]{2,1,0:T(8,128)S(1)}, u32[]{:S(2)}, u32[]{:S(2)}) collective-permute-start(f32[1,192,192]{2,1,0:T(8,128)S(1)} %slice.3), channel_id=1, source_target_pairs={{1,0},{2,1},{3,2},{4,3},{5,4},{6,5},{7,6},{8,7},{9,8},{10,9},{11,1... | collective-permute-start | bytes 442376 | tf_op jit(solution)/shard_map/ppermute | solution.py:230
  4.9 10.6 %cross.1 = (f32[32,192,192]{2,1,0:T(8,128)}, f32[32,192]{1,0:T(8,128)}) custom-call(f32[32,192]{1,0:T(8,128)} %mean.3, f32[32,192,192]{2,1,0:T(8,128)} %cov.3, f32[32,192,192]{2,1,0:T(8,128)} %dyn.1), custom_call_target="tpu_custom_call" | custom-call | flops 2717908992 | bytes 18874368 | tf_op jit(solution)/shard_map/cross/pallas_call | solution.py:237
  16.2 34.5 %fold.1 = (f32[32,192,192]{2,1,0:T(8,128)}, f32[32,192,192]{2,1,0:T(8,128)}, f32[32,192]{1,0:T(8,128)}, f32[592,128]{1,0:T(8,128)}) custom-call(f32[1,192,192]{2,1,0:T(8,128)} %copy-done.19, f32[32,192]{1,0:T(8,128)} %mean.3, f32[32,192,192]{2,1,0:T(8,128)} %cov.3, f32[32,192,192]{2,1,0:T(8,128)} %get-tuple-element.15.cross, ...), custom_call_target="tpu_custom_call" | custom-call | flops 13589544960 | bytes 31457280 | tf_op jit(solution)/shard_map/fold/pallas_call | solution.py:251
  51.4 1.1 collective-permute-done.1.other
  53.2 2.6 %pair.1 = (f32[592,128]{1,0:T(8,128)}, f32[296,128]{1,0:T(8,128)}, f32[592,128]{1,0:T(8,128)}) custom-call(s32[2]{0:T(128)} %pad_add_fusion.3.place, f32[592,128]{1,0:T(8,128)} %get-tuple-element.17.own, f32[592,128]{1,0:T(8,128)} %copy-done), custom_call_target="tpu_custom_call" | custom-call | flops 127401984 | bytes 1212416 | tf_op jit(solution)/shard_map/pair/pallas_call | solution.py:274
  55.8 1.7 %collective-permute-start.6 = (f32[296,128]{1,0:T(8,128)}, f32[296,128]{1,0:T(8,128)S(1)}, u32[]{:S(2)}, u32[]{:S(2)}) collective-permute-start(f32[296,128]{1,0:T(8,128)} %get-tuple-element.20), channel_id=1, source_target_pairs={{6,0},{7,1},{0,2},{1,3},{2,4},{3,5},{4,6},{5,7},{14,8},{15,9},{8,1... | collective-permute-start | bytes 454664 | tf_op jit(solution)/shard_map/ppermute | solution.py:292
  57.5 3.3 %collective-permute-start.4 = (f32[296,128]{1,0:T(8,128)}, f32[296,128]{1,0:T(8,128)S(1)}, u32[]{:S(2)}, u32[]{:S(2)}) collective-permute-start(f32[296,128]{1,0:T(8,128)} %get-tuple-element.20), channel_id=1, source_target_pairs={{4,0},{5,1},{6,2},{7,3},{0,4},{1,5},{2,6},{3,7},{12,8},{13,9},{14,... | collective-permute-start | bytes 454664 | tf_op jit(solution)/shard_map/ppermute | solution.py:292
  61.6 2.5 %collective-permute-done.6.refs_4_ = f32[296,128]{1,0:T(8,128)S(1)} collective-permute-done((f32[296,128]{1,0:T(8,128)}, f32[296,128]{1,0:T(8,128)S(1)}, u32[]{:S(2)}, u32[]{:S(2)}) %collective-permute-start.6) | collective-permute-done | bytes 151584 | tf_op jit(solution)/shard_map/ppermute | solution.py:292
  64.8 3.5 %collective-permute-done.4.refs_2_ = f32[296,128]{1,0:T(8,128)S(1)} collective-permute-done((f32[296,128]{1,0:T(8,128)}, f32[296,128]{1,0:T(8,128)S(1)}, u32[]{:S(2)}, u32[]{:S(2)}) %collective-permute-start.4) | collective-permute-done | bytes 151584 | tf_op jit(solution)/shard_map/ppermute | solution.py:292
  68.2 0.9 collective-permute-start.5
  71.2 3.7 %quad.2 = (f32[592,128]{1,0:T(8,128)}, f32[296,128]{1,0:T(8,128)}) custom-call(s32[2]{0:T(128)} %pad_add_fusion.2.place, f32[592,128]{1,0:T(8,128)} %get-tuple-element.19.own, f32[296,128]{1,0:T(8,128)} %copy-done.3, f32[296,128]{1,0:T(8,128)} %copy-done.6, f32[296,128]{1,0:T(8,128)} %copy-done.2, f32[296,128]{1,0:T(8,128)} %copy-done.5, ...), custom_call_target="tpu_custom_call" | custom-call | flops 382205952 | bytes 1818624 | tf_op jit(solution)/shard_map/quad/pallas_call | solution.py:299
  74.9 2.3 %collective-permute-start.12 = (f32[296,128]{1,0:T(8,128)}, f32[296,128]{1,0:T(8,128)S(1)}, u32[]{:S(2)}, u32[]{:S(2)}) collective-permute-start(f32[296,128]{1,0:T(8,128)} %get-tuple-element.22), channel_id=1, source_target_pairs={{24,0},{25,1},{26,2},{27,3},{28,4},{29,5},{30,6},{31,7},{0,8},{1,9... | collective-permute-start | bytes 454664 | tf_op jit(solution)/shard_map/ppermute | solution.py:292
  77.2 2.7 %collective-permute-start.10 = (f32[296,128]{1,0:T(8,128)}, f32[296,128]{1,0:T(8,128)S(1)}, u32[]{:S(2)}, u32[]{:S(2)}) collective-permute-start(f32[296,128]{1,0:T(8,128)} %get-tuple-element.22), channel_id=1, source_target_pairs={{16,0},{17,1},{18,2},{19,3},{20,4},{21,5},{22,6},{23,7},{24,8},{25... | collective-permute-start | bytes 454664 | tf_op jit(solution)/shard_map/ppermute | solution.py:292
  80.9 2.2 %collective-permute-done.12.refs_4_ = f32[296,128]{1,0:T(8,128)S(1)} collective-permute-done((f32[296,128]{1,0:T(8,128)}, f32[296,128]{1,0:T(8,128)S(1)}, u32[]{:S(2)}, u32[]{:S(2)}) %collective-permute-start.12) | collective-permute-done | bytes 151584 | tf_op jit(solution)/shard_map/ppermute | solution.py:292
  83.9 3.3 %collective-permute-done.10.refs_2_ = f32[296,128]{1,0:T(8,128)S(1)} collective-permute-done((f32[296,128]{1,0:T(8,128)}, f32[296,128]{1,0:T(8,128)S(1)}, u32[]{:S(2)}, u32[]{:S(2)}) %collective-permute-start.10) | collective-permute-done | bytes 151584 | tf_op jit(solution)/shard_map/ppermute | solution.py:292
  87.2 1.2 collective-permute-start.11
  90.4 3.7 %quad.3 = (f32[592,128]{1,0:T(8,128)}, f32[296,128]{1,0:T(8,128)}) custom-call(s32[2]{0:T(128)} %pad_add_fusion.1.place, f32[592,128]{1,0:T(8,128)} %get-tuple-element.21.own, f32[296,128]{1,0:T(8,128)} %copy-done.9, f32[296,128]{1,0:T(8,128)} %copy-done.12, f32[296,128]{1,0:T(8,128)} %copy-done.8, f32[296,128]{1,0:T(8,128)} %copy-done.11, ...), custom_call_target="tpu_custom_call" | custom-call | flops 382205952 | bytes 1818624 | tf_op jit(solution)/shard_map/quad/pallas_call | solution.py:299
  94.1 1.3 collective-permute-start.18
  95.4 1.3 collective-permute-start.16
  96.7 1.3 collective-permute-start.14
  98.0 8.9 %collective-permute-done.18.refs_4_ = f32[296,128]{1,0:T(8,128)S(1)} collective-permute-done((f32[296,128]{1,0:T(8,128)}, f32[296,128]{1,0:T(8,128)S(1)}, u32[]{:S(2)}, u32[]{:S(2)}) %collective-permute-start.18) | collective-permute-done | bytes 151584 | tf_op jit(solution)/shard_map/ppermute | solution.py:292
  109.0 4.1 %join.2.near = f32[592,128]{1,0:T(8,128)} custom-call(s32[2]{0:T(128)} %pad_add_fusion.2.place, f32[592,128]{1,0:T(8,128)} %get-tuple-element.18.near, f32[592,128]{1,0:T(8,128)} %get-tuple-element.19.own, f32[296,128]{1,0:T(8,128)} %copy-done.3, f32[296,128]{1,0:T(8,128)} %copy-done.6, f32[296,128]{1,0:T(8,128)} %copy-done.2, f32[296,128]{1,0:T(8,128)} %copy-done.5, ...), custom_call_target="tpu_custom_call" | custom-call | flops 382205952 | bytes 1818624 | tf_op jit(solution)/shard_map/join/pallas_call | solution.py:309
  113.1 4.1 %join.3.near = f32[592,128]{1,0:T(8,128)} custom-call(s32[2]{0:T(128)} %pad_add_fusion.1.place, f32[592,128]{1,0:T(8,128)} %join.2.near, f32[592,128]{1,0:T(8,128)} %get-tuple-element.21.own, f32[296,128]{1,0:T(8,128)} %copy-done.9, f32[296,128]{1,0:T(8,128)} %copy-done.12, f32[296,128]{1,0:T(8,128)} %copy-done.8, f32[296,128]{1,0:T(8,128)} %copy-done.11, ...), custom_call_target="tpu_custom_call" | custom-call | flops 382205952 | bytes 1818624 | tf_op jit(solution)/shard_map/join/pallas_call | solution.py:309
  118.0 14.2 %finish.1 = (f32[32,192]{1,0:T(8,128)}, f32[32,192,192]{2,1,0:T(8,128)}) custom-call(s32[2]{0:T(128)} %pad_add_fusion.place, f32[592,128]{1,0:T(8,128)} %join.3.near, f32[592,128]{1,0:T(8,128)} %get-tuple-element.23.own, f32[296,128]{1,0:T(8,128)} %copy-done.15, f32[296,128]{1,0:T(8,128)} %copy-done.18, f32[296,128]{1,0:T(8,128)} %copy-done.14, ...), custom_call_target="tpu_custom_call" | custom-call | flops 2717908992 | bytes 18874368 | tf_op jit(solution)/shard_map/finish/pallas_call | solution.py:323
  (69 shorter events, 13.0 us)
Async XLA Ops:
  1.6 13.9 %collective-permute-start = (f32[1,192,192]{2,1,0:T(8,128)S(1)}, f32[1,192,192]{2,1,0:T(8,128)S(1)}, u32[]{:S(2)}, u32[]{:S(2)}) collective-permute-start(f32[1,192,192]{2,1,0:T(8,128)S(1)} %slice.3), channel_id=1, source_target_pairs={{1,0},{2,1},{3,2},{4,3},{5,4},{6,5},{7,6},{8,7},{9,8},{10,9},{11,1... | collective-permute-start | bytes 442376 | tf_op jit(solution)/shard_map/ppermute | solution.py:230
  50.6 1.9 %collective-permute-start.1 = (f32[592,128]{1,0:T(8,128)}, f32[592,128]{1,0:T(8,128)S(1)}, u32[]{:S(2)}, u32[]{:S(2)}) collective-permute-start(f32[592,128]{1,0:T(8,128)} %get-tuple-element.17.own), channel_id=1, source_target_pairs={{0,1},{1,0},{2,3},{3,2},{4,5},{5,4},{6,7},{7,6},{8,9},{9,8},{10,11... | collective-permute-start | bytes 909320 | tf_op jit(solution)/shard_map/ppermute | solution.py:272
  55.8 8.2 %collective-permute-start.6 = (f32[296,128]{1,0:T(8,128)}, f32[296,128]{1,0:T(8,128)S(1)}, u32[]{:S(2)}, u32[]{:S(2)}) collective-permute-start(f32[296,128]{1,0:T(8,128)} %get-tuple-element.20), channel_id=1, source_target_pairs={{6,0},{7,1},{0,2},{1,3},{2,4},{3,5},{4,6},{5,7},{14,8},{15,9},{8,1... | collective-permute-start | bytes 454664 | tf_op jit(solution)/shard_map/ppermute | solution.py:292
  57.5 10.7 %collective-permute-start.4 = (f32[296,128]{1,0:T(8,128)}, f32[296,128]{1,0:T(8,128)S(1)}, u32[]{:S(2)}, u32[]{:S(2)}) collective-permute-start(f32[296,128]{1,0:T(8,128)} %get-tuple-element.20), channel_id=1, source_target_pairs={{4,0},{5,1},{6,2},{7,3},{0,4},{1,5},{2,6},{3,7},{12,8},{13,9},{14,... | collective-permute-start | bytes 454664 | tf_op jit(solution)/shard_map/ppermute | solution.py:292
  60.8 8.3 %collective-permute-start.2 = (f32[296,128]{1,0:T(8,128)}, f32[296,128]{1,0:T(8,128)S(1)}, u32[]{:S(2)}, u32[]{:S(2)}) collective-permute-start(f32[296,128]{1,0:T(8,128)} %get-tuple-element.20), channel_id=1, source_target_pairs={{2,0},{3,1},{4,2},{5,3},{6,4},{7,5},{0,6},{1,7},{10,8},{11,9},{12,... | collective-permute-start | bytes 454664 | tf_op jit(solution)/shard_map/ppermute | solution.py:292
  64.1 6.0 %collective-permute-start.7 = (f32[296,128]{1,0:T(8,128)S(1)}, f32[296,128]{1,0:T(8,128)S(1)}, u32[]{:S(2)}, u32[]{:S(2)}) collective-permute-start(f32[296,128]{1,0:T(8,128)S(1)} %collective-permute-done.6.refs_4_), channel_id=1, source_target_pairs={{0,1},{1,0},{2,3},{3,2},{4,5},{5,4},{6,7},{7,6},{8,9},{9,8},{10,11... | collective-permute-start | bytes 454664 | tf_op jit(solution)/shard_map/ppermute | solution.py:272
  68.2 2.0 %collective-permute-start.5 = (f32[296,128]{1,0:T(8,128)S(1)}, f32[296,128]{1,0:T(8,128)S(1)}, u32[]{:S(2)}, u32[]{:S(2)}) collective-permute-start(f32[296,128]{1,0:T(8,128)S(1)} %collective-permute-done.4.refs_2_), channel_id=1, source_target_pairs={{0,1},{1,0},{2,3},{3,2},{4,5},{5,4},{6,7},{7,6},{8,9},{9,8},{10,11... | collective-permute-start | bytes 454664 | tf_op jit(solution)/shard_map/ppermute | solution.py:272
  69.2 1.4 %collective-permute-start.3 = (f32[296,128]{1,0:T(8,128)S(1)}, f32[296,128]{1,0:T(8,128)S(1)}, u32[]{:S(2)}, u32[]{:S(2)}) collective-permute-start(f32[296,128]{1,0:T(8,128)S(1)} %collective-permute-done.2.refs_0_), channel_id=1, source_target_pairs={{0,1},{1,0},{2,3},{3,2},{4,5},{5,4},{6,7},{7,6},{8,9},{9,8},{10,11... | collective-permute-start | bytes 454664 | tf_op jit(solution)/shard_map/ppermute | solution.py:272
  74.9 8.1 %collective-permute-start.12 = (f32[296,128]{1,0:T(8,128)}, f32[296,128]{1,0:T(8,128)S(1)}, u32[]{:S(2)}, u32[]{:S(2)}) collective-permute-start(f32[296,128]{1,0:T(8,128)} %get-tuple-element.22), channel_id=1, source_target_pairs={{24,0},{25,1},{26,2},{27,3},{28,4},{29,5},{30,6},{31,7},{0,8},{1,9... | collective-permute-start | bytes 454664 | tf_op jit(solution)/shard_map/ppermute | solution.py:292
  77.2 9.9 %collective-permute-start.10 = (f32[296,128]{1,0:T(8,128)}, f32[296,128]{1,0:T(8,128)S(1)}, u32[]{:S(2)}, u32[]{:S(2)}) collective-permute-start(f32[296,128]{1,0:T(8,128)} %get-tuple-element.22), channel_id=1, source_target_pairs={{16,0},{17,1},{18,2},{19,3},{20,4},{21,5},{22,6},{23,7},{24,8},{25... | collective-permute-start | bytes 454664 | tf_op jit(solution)/shard_map/ppermute | solution.py:292
  80.0 8.3 %collective-permute-start.8 = (f32[296,128]{1,0:T(8,128)}, f32[296,128]{1,0:T(8,128)S(1)}, u32[]{:S(2)}, u32[]{:S(2)}) collective-permute-start(f32[296,128]{1,0:T(8,128)} %get-tuple-element.22), channel_id=1, source_target_pairs={{8,0},{9,1},{10,2},{11,3},{12,4},{13,5},{14,6},{15,7},{16,8},{17,9... | collective-permute-start | bytes 454664 | tf_op jit(solution)/shard_map/ppermute | solution.py:292
  83.1 6.7 %copy-start.7 = (f32[296,128]{1,0:T(8,128)}, f32[296,128]{1,0:T(8,128)S(1)}, u32[]{:S(2)}) copy-start(f32[296,128]{1,0:T(8,128)S(1)} %collective-permute-done.12.refs_4_) | copy-start | bytes 454660
  83.1 5.9 %collective-permute-start.13 = (f32[296,128]{1,0:T(8,128)S(1)}, f32[296,128]{1,0:T(8,128)S(1)}, u32[]{:S(2)}, u32[]{:S(2)}) collective-permute-start(f32[296,128]{1,0:T(8,128)S(1)} %collective-permute-done.12.refs_4_), channel_id=1, source_target_pairs={{0,1},{1,0},{2,3},{3,2},{4,5},{5,4},{6,7},{7,6},{8,9},{9,8},{10,11... | collective-permute-start | bytes 454664 | tf_op jit(solution)/shard_map/ppermute | solution.py:272
  87.2 2.2 %collective-permute-start.11 = (f32[296,128]{1,0:T(8,128)S(1)}, f32[296,128]{1,0:T(8,128)S(1)}, u32[]{:S(2)}, u32[]{:S(2)}) collective-permute-start(f32[296,128]{1,0:T(8,128)S(1)} %collective-permute-done.10.refs_2_), channel_id=1, source_target_pairs={{0,1},{1,0},{2,3},{3,2},{4,5},{5,4},{6,7},{7,6},{8,9},{9,8},{10,11... | collective-permute-start | bytes 454664 | tf_op jit(solution)/shard_map/ppermute | solution.py:272
  88.3 1.4 %collective-permute-start.9 = (f32[296,128]{1,0:T(8,128)S(1)}, f32[296,128]{1,0:T(8,128)S(1)}, u32[]{:S(2)}, u32[]{:S(2)}) collective-permute-start(f32[296,128]{1,0:T(8,128)S(1)} %collective-permute-done.8.refs_0_), channel_id=1, source_target_pairs={{0,1},{1,0},{2,3},{3,2},{4,5},{5,4},{6,7},{7,6},{8,9},{9,8},{10,11... | collective-permute-start | bytes 454664 | tf_op jit(solution)/shard_map/ppermute | solution.py:272
  94.1 12.8 %collective-permute-start.18 = (f32[296,128]{1,0:T(8,128)}, f32[296,128]{1,0:T(8,128)S(1)}, u32[]{:S(2)}, u32[]{:S(2)}) collective-permute-start(f32[296,128]{1,0:T(8,128)} %get-tuple-element.24), channel_id=1, source_target_pairs={{96,0},{97,1},{98,2},{99,3},{100,4},{101,5},{102,6},{103,7},{104,8... | collective-permute-start | bytes 454664 | tf_op jit(solution)/shard_map/ppermute | solution.py:292
  95.4 12.4 %collective-permute-start.16 = (f32[296,128]{1,0:T(8,128)}, f32[296,128]{1,0:T(8,128)S(1)}, u32[]{:S(2)}, u32[]{:S(2)}) collective-permute-start(f32[296,128]{1,0:T(8,128)} %get-tuple-element.24), channel_id=1, source_target_pairs={{64,0},{65,1},{66,2},{67,3},{68,4},{69,5},{70,6},{71,7},{72,8},{73... | collective-permute-start | bytes 454664 | tf_op jit(solution)/shard_map/ppermute | solution.py:292
  96.7 11.2 %collective-permute-start.14 = (f32[296,128]{1,0:T(8,128)}, f32[296,128]{1,0:T(8,128)S(1)}, u32[]{:S(2)}, u32[]{:S(2)}) collective-permute-start(f32[296,128]{1,0:T(8,128)} %get-tuple-element.24), channel_id=1, source_target_pairs={{32,0},{33,1},{34,2},{35,3},{36,4},{37,5},{38,6},{39,7},{40,8},{41... | collective-permute-start | bytes 454664 | tf_op jit(solution)/shard_map/ppermute | solution.py:292
  106.9 10.3 %copy-start.13 = (f32[296,128]{1,0:T(8,128)}, f32[296,128]{1,0:T(8,128)S(1)}, u32[]{:S(2)}) copy-start(f32[296,128]{1,0:T(8,128)S(1)} %collective-permute-done.18.refs_4_) | copy-start | bytes 454660
  106.9 10.3 %collective-permute-start.19 = (f32[296,128]{1,0:T(8,128)S(1)}, f32[296,128]{1,0:T(8,128)S(1)}, u32[]{:S(2)}, u32[]{:S(2)}) collective-permute-start(f32[296,128]{1,0:T(8,128)S(1)} %collective-permute-done.18.refs_4_), channel_id=1, source_target_pairs={{0,1},{1,0},{2,3},{3,2},{4,5},{5,4},{6,7},{7,6},{8,9},{9,8},{10,11... | collective-permute-start | bytes 454664 | tf_op jit(solution)/shard_map/ppermute | solution.py:272
  107.8 9.5 %copy-start.14 = (f32[296,128]{1,0:T(8,128)}, f32[296,128]{1,0:T(8,128)S(1)}, u32[]{:S(2)}) copy-start(f32[296,128]{1,0:T(8,128)S(1)} %collective-permute-done.16.refs_2_) | copy-start | bytes 454660
  107.8 9.4 %collective-permute-start.17 = (f32[296,128]{1,0:T(8,128)S(1)}, f32[296,128]{1,0:T(8,128)S(1)}, u32[]{:S(2)}, u32[]{:S(2)}) collective-permute-start(f32[296,128]{1,0:T(8,128)S(1)} %collective-permute-done.16.refs_2_), channel_id=1, source_target_pairs={{0,1},{1,0},{2,3},{3,2},{4,5},{5,4},{6,7},{7,6},{8,9},{9,8},{10,11... | collective-permute-start | bytes 454664 | tf_op jit(solution)/shard_map/ppermute | solution.py:272
  107.9 9.4 %copy-start.15 = (f32[296,128]{1,0:T(8,128)}, f32[296,128]{1,0:T(8,128)S(1)}, u32[]{:S(2)}) copy-start(f32[296,128]{1,0:T(8,128)S(1)} %collective-permute-done.14.refs_0_) | copy-start | bytes 454660
  107.9 9.3 %collective-permute-start.15 = (f32[296,128]{1,0:T(8,128)S(1)}, f32[296,128]{1,0:T(8,128)S(1)}, u32[]{:S(2)}, u32[]{:S(2)}) collective-permute-start(f32[296,128]{1,0:T(8,128)S(1)} %collective-permute-done.14.refs_0_), channel_id=1, source_target_pairs={{0,1},{1,0},{2,3},{3,2},{4,5},{5,4},{6,7},{7,6},{8,9},{9,8},{10,11... | collective-permute-start | bytes 454664 | tf_op jit(solution)/shard_map/ppermute | solution.py:272
  (16 other events, 21.8 us)

commit v2 on v1

--- a/solution.py
+++ b/solution.py
@@ -1,3 +1,5 @@
+import functools
+
 import jax
 import jax.numpy as jnp
 from jax import lax
@@ -29,11 +31,18 @@
     return high, (x - high.astype(F32)).astype(jnp.bfloat16)
 
 
+def filled(x, dim):
+    shape = list(x.shape)
+    shape[dim] = 256 - W
+    return jnp.concatenate([x, jnp.zeros(shape, x.dtype)], dim)
+
+
 def three(a, b, side):
-    def part(x, y):
-        return lax.dot_general(x, y, (((1,), (side,)), ((), ())), preferred_element_type=F32)
-
-    return part(a[0], b[0]) + (part(a[0], b[1]) + part(a[1], b[0]))
+    high, low = filled(a[0], 1), filled(a[1], 1)
+    left = jnp.concatenate([high, high, low], 1)
+    high, low = filled(b[0], side), filled(b[1], side)
+    right = jnp.concatenate([high, low, high], side)
+    return lax.dot_general(left, right, (((1,), (side,)), ((), ())), preferred_element_type=F32)
 
 
 def packed(e, l, u, ref):
@@ -130,7 +139,7 @@
 
 
 def pair_kernel(place, own, other, total, half, after):
-    low = place[1] == 0
+    low = place[0] == 0
 
     @pl.when(low)
     def _():
@@ -142,11 +151,10 @@
         packed(eye(), jnp.zeros((W, W), F32), jnp.zeros((16, W), F32), after)
         packed(*composed(unpacked(other), unpacked(own)), total)
 
-    half[...] = total[pl.ds(pl.multiple_of(place[1] * HALF, 8), HALF), :]
-
-
-def arrange(place, own, halves, ordered):
-    spot, core = place[0], place[1]
+    half[...] = total[pl.ds(pl.multiple_of(place[0] * HALF, 8), HALF), :]
+
+
+def arrange(core, spot, own, halves, ordered):
     ordered[spot] = own[...]
     mine = pl.multiple_of(core * HALF, 8)
     theirs = pl.multiple_of((1 - core) * HALF, 8)
@@ -156,46 +164,42 @@
         ordered[slot, pl.ds(theirs, HALF), :] = halves[2 * k + 1][...]
 
 
-def quad_kernel(place, own, *refs):
-    halves, (total, half, ordered) = refs[:6], refs[6:]
-    arrange(place, own, halves, ordered)
+def quad_kernel(level, place, near, follow, own, *refs):
+    halves, (total, half, after, joined, ordered) = refs[:6], refs[6:]
+    spot = place[level]
+    arrange(place[0], spot, own, halves, ordered)
     parts = [unpacked(ordered.at[k]) for k in range(4)]
     early, late = composed(parts[0], parts[1]), composed(parts[2], parts[3])
-    packed(*composed(early, late), total)
-    half[...] = total[pl.ds(pl.multiple_of(place[1] * HALF, 8), HALF), :]
-
-
-def join_kernel(place, near, own, *refs):
-    halves, (joined, ordered) = refs[:6], refs[6:]
-    arrange(place, own, halves, ordered)
-    joined[...] = near[...]
-    for k in (1, 2, 3):
-
-        @pl.when(k > place[0])
-        def _():
-            packed(*composed(unpacked(joined), unpacked(ordered.at[k])), joined)
-
-
-def advance(element, cov, mean):
-    e, l, u = unpacked(element)
-    cov[...], mean[...] = applied(split(e), l, u, split(cov[...]), mean[...])
-
-
-def finish_kernel(place, near, own, *refs):
+    whole = composed(early, late)
+    rest = composed(parts[1], late)
+    joint = composed(unpacked(near), unpacked(follow))
+    packed(*whole, total)
+    packed(*joint, joined)
+    half[...] = total[pl.ds(pl.multiple_of(place[0] * HALF, 8), HALF), :]
+    last = (eye(), jnp.zeros((W, W), F32), jnp.zeros((16, W), F32))
+    picked = [
+        jnp.where(spot == 0, r, jnp.where(spot == 1, l, jnp.where(spot == 2, p, z)))
+        for r, l, p, z in zip(rest, late, parts[3], last)
+    ]
+    packed(*picked, after)
+
+
+def finish_kernel(place, near, follow, own, *refs):
     halves, (e_all, l_all, u_all, mean_out, cov_out, ordered, cov_in, mean_in) = refs[:6], refs[6:]
 
     @pl.when(pl.program_id(0) == 0)
     def _():
-        arrange(place, own, halves, ordered)
-        cov_in[...] = jnp.zeros((W, W), F32)
-        mean_in[...] = jnp.zeros((16, W), F32)
-        for k in (3, 2, 1):
-
-            @pl.when(k > place[0])
-            def _():
-                advance(ordered.at[k], cov_in, mean_in)
-
-        advance(near, cov_in, mean_in)
+        spot = place[3]
+        arrange(place[0], spot, own, halves, ordered)
+        cov, mean = jnp.zeros((W, W), F32), jnp.zeros((16, W), F32)
+        joint = composed(unpacked(near), unpacked(follow))
+        _, l, u = unpacked(ordered.at[3])
+        cov, mean = jnp.where(spot < 3, l, cov), jnp.where(spot < 3, u, mean)
+        for k in (2, 1):
+            e, l, u = unpacked(ordered.at[k])
+            new_cov, new_mean = applied(split(e), l, u, split(cov), mean)
+            cov, mean = jnp.where(spot < k, new_cov, cov), jnp.where(spot < k, new_mean, mean)
+        cov_in[...], mean_in[...] = applied(split(joint[0]), joint[1], joint[2], split(cov), mean)
 
     cov, mean = split(cov_in[...]), mean_in[...]
     for j in range(STEPS):
@@ -265,8 +269,9 @@
         name="fold",
     )(following, filtered_mean, filtered_cov, cross, moved, predicted_precision)
 
-    def place(stride):
-        return jnp.stack([lax.rem(lax.div(here, stride), 4), lax.rem(here, 2)])
+    place = jnp.stack(
+        [lax.rem(here, 2)] + [lax.rem(lax.div(here, stride), 4) for stride in (2, 8, 32)]
+    )
 
     def other_core(part):
         return lax.ppermute(part, "tm", [(i, i ^ 1) for i in range(peers)])
@@ -279,7 +284,7 @@
         compiler_params=PARAMS,
         cost_estimate=cost(3, 3, 4 * ELEMENT),
         name="pair",
-    )(place(1), total, other_core(total))
+    )(place, total, other_core(total))
 
     def gathered(half, stride, later_only):
         got = [None] * 3
@@ -293,29 +298,20 @@
             got[k - 1] = (mine, other_core(mine))
         return [part for two in got for part in two]
 
-    for stride in (2, 8):
+    follow = near
+    for level, stride in ((1, 2), (2, 8)):
         parts = gathered(half, stride, False)
-        own = total
-        total, half = pl.pallas_call(
-            quad_kernel,
-            in_specs=[SCALAR] + [WHOLE] * 7,
-            out_specs=[WHOLE, WHOLE],
-            out_shape=[struct(ROWS, 128), struct(HALF, 128)],
+        total, half, after, joined = pl.pallas_call(
+            functools.partial(quad_kernel, level),
+            in_specs=[SCALAR] + [WHOLE] * 9,
+            out_specs=[WHOLE] * 4,
+            out_shape=[struct(ROWS, 128), struct(HALF, 128), struct(ROWS, 128), struct(ROWS, 128)],
             scratch_shapes=[pltpu.VMEM((4, ROWS, 128), F32)],
             compiler_params=PARAMS,
-            cost_estimate=cost(9, 3, 6 * ELEMENT),
+            cost_estimate=cost(15, 3, 10 * ELEMENT),
             name="quad",
-        )(place(stride), own, *parts)
-        near = pl.pallas_call(
-            join_kernel,
-            in_specs=[SCALAR] + [WHOLE] * 8,
-            out_specs=WHOLE,
-            out_shape=struct(ROWS, 128),
-            scratch_shapes=[pltpu.VMEM((4, ROWS, 128), F32)],
-            compiler_params=PARAMS,
-            cost_estimate=cost(9, 3, 6 * ELEMENT),
-            name="join",
-        )(place(stride), near, own, *parts)
+        )(place, near, follow, total, *parts)
+        near, follow = (near if stride == 2 else joined), after
 
     parts = gathered(half, 32, True)
     flat = pl.BlockSpec((ROWS, 128), lambda i: (0, 0))
@@ -323,7 +319,7 @@
     return pl.pallas_call(
         finish_kernel,
         grid=(blocks,),
-        in_specs=[SCALAR] + [flat] * 2 + [flat_half] * 6 + [mat, mat, vec],
+        in_specs=[SCALAR] + [flat] * 3 + [flat_half] * 6 + [mat, mat, vec],
         out_specs=[vec, mat],
         out_shape=[struct(count, W), struct(count, W, W)],
         scratch_shapes=[
@@ -334,7 +330,7 @@
         compiler_params=PARAMS,
         cost_estimate=cost(2 * count, 3, 3 * matrices),
         name="finish",
-    )(place(32), near, total, *parts, e_all, l_all, u_all)
+    )(place, near, follow, total, *parts, e_all, l_all, u_all)
 
 
 def solution(mesh):

time: 133 us -> 126 us (0.947)
  Pallas kernels: 77.5 us -> 71 us
  waiting for transfers between devices: 22.8 us -> 25 us
  other arithmetic: 2.44 us -> 0.66 us
    pallas_call x4 -> x2, Pallas kernels: 15.7 us -> 9.38 us  [on_device(): pl.pallas_call(functools.partial(quad_kernel, level), in_specs=[SCALAR] +...]
    ppermute x10, waiting for transfers between devices: 2.38 us -> 4.56 us  [other_core(): return lax.ppermute(part, 'tm', [(i, i ^ 1) for i in range(peers)])]
    another operation x4 -> x1, other arithmetic: 2.44 us -> 0.66 us  [on_device(): jnp.stack([lax.rem(here, 2)] + [lax.rem(lax.div(here, stride), 4) for str...]
  transfers between devices with their start and end apart: 20 -> 20, of which waited for: 10 -> 13; matrix products, arithmetic and copies ran while one was open for 2% -> 1% of each run, Pallas kernels for 14% -> 8%
where the time goes in v2:
time: 126 us
  Pallas kernels  71 us (56%)
  waiting for transfers between devices  25 us (20%)
  starting transfers between devices  24.3 us (19%)
  local copies, waits for them, and re-layouts  4.32 us (3%)
    pallas_call x1, Pallas kernels, on_device(): pl.pallas_call(fold_kernel, grid=(blocks,), in_specs=[once, down, down3,...  34.4 us
    ppermute x9, waiting for transfers between devices, gathered(): mine = lax.ppermute(half, 'tm', pairs)  20.4 us
    ppermute x9, starting transfers between devices, gathered(): mine = lax.ppermute(half, 'tm', pairs)  15.5 us
    pallas_call x1, Pallas kernels, on_device(): pl.pallas_call(finish_kernel, grid=(blocks,), in_specs=[SCALAR] + [flat]...  14.1 us
    pallas_call x1, Pallas kernels, on_device(): pl.pallas_call(cross_kernel, grid=(blocks,), in_specs=[vec, mat, mat], ou...  10.6 us
    pallas_call x2, Pallas kernels, on_device(): pl.pallas_call(functools.partial(quad_kernel, level), in_specs=[SCALAR] +...  9.38 us
    ppermute x10, starting transfers between devices, other_core(): return lax.ppermute(part, 'tm', [(i, i ^ 1) for i in range(peers)])  5.48 us
    ppermute x10, waiting for transfers between devices, other_core(): return lax.ppermute(part, 'tm', [(i, i ^ 1) for i in range(peers)])  4.56 us
  transfers between devices with their start and end apart: 20, of which 13 were waited for; matrix products, arithmetic and copies ran while one was open for 1% of the time, Pallas kernels for 8%

profile of v2, /device:TPU:1, one launch (start us, length us, event | category | flops | bytes accessed | tf_op | source)
XLA Modules:
  0.0 126.1 jit_solution(10738199011989153325)
XLA Ops:
  0.6 0.9 slice.3
  1.6 3.3 %collective-permute-start = (f32[1,192,192]{2,1,0:T(8,128)S(1)}, f32[1,192,192]{2,1,0:T(8,128)S(1)}, u32[]{:S(2)}, u32[]{:S(2)}) collective-permute-start(f32[1,192,192]{2,1,0:T(8,128)S(1)} %slice.3), channel_id=1, source_target_pairs={{1,0},{2,1},{3,2},{4,3},{5,4},{6,5},{7,6},{8,7},{9,8},{10,9},{11,1... | collective-permute-start | bytes 442376 | tf_op jit(solution)/shard_map/ppermute | solution.py:234
  4.9 10.6 %cross.1 = (f32[32,192,192]{2,1,0:T(8,128)}, f32[32,192]{1,0:T(8,128)}) custom-call(f32[32,192]{1,0:T(8,128)} %mean.3, f32[32,192,192]{2,1,0:T(8,128)} %cov.3, f32[32,192,192]{2,1,0:T(8,128)} %dyn.1), custom_call_target="tpu_custom_call" | custom-call | flops 2717908992 | bytes 18874368 | tf_op jit(solution)/shard_map/cross/pallas_call | solution.py:241
  16.2 34.4 %fold.1 = (f32[32,192,192]{2,1,0:T(8,128)}, f32[32,192,192]{2,1,0:T(8,128)}, f32[32,192]{1,0:T(8,128)}, f32[592,128]{1,0:T(8,128)}) custom-call(f32[1,192,192]{2,1,0:T(8,128)} %copy-done.7, f32[32,192]{1,0:T(8,128)} %mean.3, f32[32,192,192]{2,1,0:T(8,128)} %cov.3, f32[32,192,192]{2,1,0:T(8,128)} %get-tuple-element.18.cross, ...), custom_call_target="tpu_custom_call" | custom-call | flops 13589544960 | bytes 31457280 | tf_op jit(solution)/shard_map/fold/pallas_call | solution.py:255
  51.3 1.1 collective-permute-done.1.other
  53.1 2.6 %pair.1 = (f32[592,128]{1,0:T(8,128)}, f32[296,128]{1,0:T(8,128)}, f32[592,128]{1,0:T(8,128)}) custom-call(s32[4]{0:T(128)} %pad_add_fusion.place, f32[592,128]{1,0:T(8,128)} %get-tuple-element.20.own, f32[592,128]{1,0:T(8,128)} %copy-done), custom_call_target="tpu_custom_call" | custom-call | flops 127401984 | bytes 1212416 | tf_op jit(solution)/shard_map/pair/pallas_call | solution.py:279
  55.7 1.7 %collective-permute-start.6 = (f32[296,128]{1,0:T(8,128)}, f32[296,128]{1,0:T(8,128)S(1)}, u32[]{:S(2)}, u32[]{:S(2)}) collective-permute-start(f32[296,128]{1,0:T(8,128)} %get-tuple-element.23), channel_id=1, source_target_pairs={{6,0},{7,1},{0,2},{1,3},{2,4},{3,5},{4,6},{5,7},{14,8},{15,9},{8,1... | collective-permute-start | bytes 454664 | tf_op jit(solution)/shard_map/ppermute | solution.py:297
  57.5 3.3 %collective-permute-start.4 = (f32[296,128]{1,0:T(8,128)}, f32[296,128]{1,0:T(8,128)S(1)}, u32[]{:S(2)}, u32[]{:S(2)}) collective-permute-start(f32[296,128]{1,0:T(8,128)} %get-tuple-element.23), channel_id=1, source_target_pairs={{4,0},{5,1},{6,2},{7,3},{0,4},{1,5},{2,6},{3,7},{12,8},{13,9},{14,... | collective-permute-start | bytes 454664 | tf_op jit(solution)/shard_map/ppermute | solution.py:297
  61.5 2.5 %collective-permute-done.6.refs_4_ = f32[296,128]{1,0:T(8,128)S(1)} collective-permute-done((f32[296,128]{1,0:T(8,128)}, f32[296,128]{1,0:T(8,128)S(1)}, u32[]{:S(2)}, u32[]{:S(2)}) %collective-permute-start.6) | collective-permute-done | bytes 151584 | tf_op jit(solution)/shard_map/ppermute | solution.py:297
  64.7 3.5 %collective-permute-done.4.refs_2_ = f32[296,128]{1,0:T(8,128)S(1)} collective-permute-done((f32[296,128]{1,0:T(8,128)}, f32[296,128]{1,0:T(8,128)S(1)}, u32[]{:S(2)}, u32[]{:S(2)}) %collective-permute-start.4) | collective-permute-done | bytes 151584 | tf_op jit(solution)/shard_map/ppermute | solution.py:297
  68.2 0.9 collective-permute-start.5
  71.1 4.7 %quad.2 = (f32[592,128]{1,0:T(8,128)}, f32[296,128]{1,0:T(8,128)}, f32[592,128]{1,0:T(8,128)}, f32[592,128]{1,0:T(8,128)}) custom-call(s32[4]{0:T(128)} %pad_add_fusion.place, f32[592,128]{1,0:T(8,128)} %get-tuple-element.21.near.follow, f32[592,128]{1,0:T(8,128)} %get-tuple-element.21.near.follow, f32[592,128]{1,0:T(8,128)} %get-tuple-element.22.own, ...), custom_call_target="tpu_custom_call" | custom-call | flops 637009920 | bytes 3031040 | tf_op jit(solution)/shard_map/quad/pallas_call | solution.py:304
  75.8 2.3 %collective-permute-start.12 = (f32[296,128]{1,0:T(8,128)}, f32[296,128]{1,0:T(8,128)S(1)}, u32[]{:S(2)}, u32[]{:S(2)}) collective-permute-start(f32[296,128]{1,0:T(8,128)} %get-tuple-element.26), channel_id=1, source_target_pairs={{24,0},{25,1},{26,2},{27,3},{28,4},{29,5},{30,6},{31,7},{0,8},{1,9... | collective-permute-start | bytes 454664 | tf_op jit(solution)/shard_map/ppermute | solution.py:297
  78.1 2.7 %collective-permute-start.10 = (f32[296,128]{1,0:T(8,128)}, f32[296,128]{1,0:T(8,128)S(1)}, u32[]{:S(2)}, u32[]{:S(2)}) collective-permute-start(f32[296,128]{1,0:T(8,128)} %get-tuple-element.26), channel_id=1, source_target_pairs={{16,0},{17,1},{18,2},{19,3},{20,4},{21,5},{22,6},{23,7},{24,8},{25... | collective-permute-start | bytes 454664 | tf_op jit(solution)/shard_map/ppermute | solution.py:297
  81.7 2.2 %collective-permute-done.12.refs_4_ = f32[296,128]{1,0:T(8,128)S(1)} collective-permute-done((f32[296,128]{1,0:T(8,128)}, f32[296,128]{1,0:T(8,128)S(1)}, u32[]{:S(2)}, u32[]{:S(2)}) %collective-permute-start.12) | collective-permute-done | bytes 151584 | tf_op jit(solution)/shard_map/ppermute | solution.py:297
  84.8 3.3 %collective-permute-done.10.refs_2_ = f32[296,128]{1,0:T(8,128)S(1)} collective-permute-done((f32[296,128]{1,0:T(8,128)}, f32[296,128]{1,0:T(8,128)S(1)}, u32[]{:S(2)}, u32[]{:S(2)}) %collective-permute-start.10) | collective-permute-done | bytes 151584 | tf_op jit(solution)/shard_map/ppermute | solution.py:297
  88.1 1.2 collective-permute-start.11
  89.3 0.9 collective-permute-done.11.refs_3_
  91.3 4.7 %quad.3 = (f32[592,128]{1,0:T(8,128)}, f32[296,128]{1,0:T(8,128)}, f32[592,128]{1,0:T(8,128)}, f32[592,128]{1,0:T(8,128)}) custom-call(s32[4]{0:T(128)} %pad_add_fusion.place, f32[592,128]{1,0:T(8,128)} %get-tuple-element.21.near.follow, f32[592,128]{1,0:T(8,128)} %get-tuple-element.24.follow, f32[592,128]{1,0:T(8,128)} %get-tuple-element.25.own, ...), custom_call_target="tpu_custom_call" | custom-call | flops 637009920 | bytes 3031040 | tf_op jit(solution)/shard_map/quad/pallas_call | solution.py:304
  96.0 1.3 %collective-permute-start.18 = (f32[296,128]{1,0:T(8,128)}, f32[296,128]{1,0:T(8,128)S(1)}, u32[]{:S(2)}, u32[]{:S(2)}) collective-permute-start(f32[296,128]{1,0:T(8,128)} %get-tuple-element.30), channel_id=1, source_target_pairs={{96,0},{97,1},{98,2},{99,3},{100,4},{101,5},{102,6},{103,7},{104,8... | collective-permute-start | bytes 454664 | tf_op jit(solution)/shard_map/ppermute | solution.py:297
  97.3 1.3 %collective-permute-start.16 = (f32[296,128]{1,0:T(8,128)}, f32[296,128]{1,0:T(8,128)S(1)}, u32[]{:S(2)}, u32[]{:S(2)}) collective-permute-start(f32[296,128]{1,0:T(8,128)} %get-tuple-element.30), channel_id=1, source_target_pairs={{64,0},{65,1},{66,2},{67,3},{68,4},{69,5},{70,6},{71,7},{72,8},{73... | collective-permute-start | bytes 454664 | tf_op jit(solution)/shard_map/ppermute | solution.py:297
  98.6 1.3 %collective-permute-start.14 = (f32[296,128]{1,0:T(8,128)}, f32[296,128]{1,0:T(8,128)S(1)}, u32[]{:S(2)}, u32[]{:S(2)}) collective-permute-start(f32[296,128]{1,0:T(8,128)} %get-tuple-element.30), channel_id=1, source_target_pairs={{32,0},{33,1},{34,2},{35,3},{36,4},{37,5},{38,6},{39,7},{40,8},{41... | collective-permute-start | bytes 454664 | tf_op jit(solution)/shard_map/ppermute | solution.py:297
  99.9 8.9 %collective-permute-done.18.refs_4_ = f32[296,128]{1,0:T(8,128)S(1)} collective-permute-done((f32[296,128]{1,0:T(8,128)}, f32[296,128]{1,0:T(8,128)S(1)}, u32[]{:S(2)}, u32[]{:S(2)}) %collective-permute-start.18) | collective-permute-done | bytes 151584 | tf_op jit(solution)/shard_map/ppermute | solution.py:297
  112.0 14.1 %finish.1 = (f32[32,192]{1,0:T(8,128)}, f32[32,192,192]{2,1,0:T(8,128)}) custom-call(s32[4]{0:T(128)} %pad_add_fusion.place, f32[592,128]{1,0:T(8,128)} %get-tuple-element.27.near, f32[592,128]{1,0:T(8,128)} %get-tuple-element.28.follow, f32[592,128]{1,0:T(8,128)} %get-tuple-element.29.own, f32[296,128]{1,0:T(8,128)} %copy-done.3, f32[296,128]{1,0:T(8,128)} %copy-done.6, ...), custom_call_target="tpu_custom_call" | custom-call | flops 2717908992 | bytes 18874368 | tf_op jit(solution)/shard_map/finish/pallas_call | solution.py:319
  (64 shorter events, 11.6 us)
Async XLA Ops:
  1.6 13.9 %collective-permute-start = (f32[1,192,192]{2,1,0:T(8,128)S(1)}, f32[1,192,192]{2,1,0:T(8,128)S(1)}, u32[]{:S(2)}, u32[]{:S(2)}) collective-permute-start(f32[1,192,192]{2,1,0:T(8,128)S(1)} %slice.3), channel_id=1, source_target_pairs={{1,0},{2,1},{3,2},{4,3},{5,4},{6,5},{7,6},{8,7},{9,8},{10,9},{11,1... | collective-permute-start | bytes 442376 | tf_op jit(solution)/shard_map/ppermute | solution.py:234
  50.5 1.9 %collective-permute-start.1 = (f32[592,128]{1,0:T(8,128)}, f32[592,128]{1,0:T(8,128)S(1)}, u32[]{:S(2)}, u32[]{:S(2)}) collective-permute-start(f32[592,128]{1,0:T(8,128)} %get-tuple-element.20.own), channel_id=1, source_target_pairs={{0,1},{1,0},{2,3},{3,2},{4,5},{5,4},{6,7},{7,6},{8,9},{9,8},{10,11... | collective-permute-start | bytes 909320 | tf_op jit(solution)/shard_map/ppermute | solution.py:277
  55.7 8.2 %collective-permute-start.6 = (f32[296,128]{1,0:T(8,128)}, f32[296,128]{1,0:T(8,128)S(1)}, u32[]{:S(2)}, u32[]{:S(2)}) collective-permute-start(f32[296,128]{1,0:T(8,128)} %get-tuple-element.23), channel_id=1, source_target_pairs={{6,0},{7,1},{0,2},{1,3},{2,4},{3,5},{4,6},{5,7},{14,8},{15,9},{8,1... | collective-permute-start | bytes 454664 | tf_op jit(solution)/shard_map/ppermute | solution.py:297
  57.5 10.7 %collective-permute-start.4 = (f32[296,128]{1,0:T(8,128)}, f32[296,128]{1,0:T(8,128)S(1)}, u32[]{:S(2)}, u32[]{:S(2)}) collective-permute-start(f32[296,128]{1,0:T(8,128)} %get-tuple-element.23), channel_id=1, source_target_pairs={{4,0},{5,1},{6,2},{7,3},{0,4},{1,5},{2,6},{3,7},{12,8},{13,9},{14,... | collective-permute-start | bytes 454664 | tf_op jit(solution)/shard_map/ppermute | solution.py:297
  60.8 8.3 %collective-permute-start.2 = (f32[296,128]{1,0:T(8,128)}, f32[296,128]{1,0:T(8,128)S(1)}, u32[]{:S(2)}, u32[]{:S(2)}) collective-permute-start(f32[296,128]{1,0:T(8,128)} %get-tuple-element.23), channel_id=1, source_target_pairs={{2,0},{3,1},{4,2},{5,3},{6,4},{7,5},{0,6},{1,7},{10,8},{11,9},{12,... | collective-permute-start | bytes 454664 | tf_op jit(solution)/shard_map/ppermute | solution.py:297
  64.0 6.5 %copy-start.9 = (f32[296,128]{1,0:T(8,128)}, f32[296,128]{1,0:T(8,128)S(1)}, u32[]{:S(2)}) copy-start(f32[296,128]{1,0:T(8,128)S(1)} %collective-permute-done.6.refs_4_) | copy-start | bytes 454660
  64.0 5.4 %collective-permute-start.7 = (f32[296,128]{1,0:T(8,128)S(1)}, f32[296,128]{1,0:T(8,128)S(1)}, u32[]{:S(2)}, u32[]{:S(2)}) collective-permute-start(f32[296,128]{1,0:T(8,128)S(1)} %collective-permute-done.6.refs_4_), channel_id=1, source_target_pairs={{0,1},{1,0},{2,3},{3,2},{4,5},{5,4},{6,7},{7,6},{8,9},{9,8},{10,11... | collective-permute-start | bytes 454664 | tf_op jit(solution)/shard_map/ppermute | solution.py:277
  68.2 2.0 %collective-permute-start.5 = (f32[296,128]{1,0:T(8,128)S(1)}, f32[296,128]{1,0:T(8,128)S(1)}, u32[]{:S(2)}, u32[]{:S(2)}) collective-permute-start(f32[296,128]{1,0:T(8,128)S(1)} %collective-permute-done.4.refs_2_), channel_id=1, source_target_pairs={{0,1},{1,0},{2,3},{3,2},{4,5},{5,4},{6,7},{7,6},{8,9},{9,8},{10,11... | collective-permute-start | bytes 454664 | tf_op jit(solution)/shard_map/ppermute | solution.py:277
  69.1 1.4 %collective-permute-start.3 = (f32[296,128]{1,0:T(8,128)S(1)}, f32[296,128]{1,0:T(8,128)S(1)}, u32[]{:S(2)}, u32[]{:S(2)}) collective-permute-start(f32[296,128]{1,0:T(8,128)S(1)} %collective-permute-done.2.refs_0_), channel_id=1, source_target_pairs={{0,1},{1,0},{2,3},{3,2},{4,5},{5,4},{6,7},{7,6},{8,9},{9,8},{10,11... | collective-permute-start | bytes 454664 | tf_op jit(solution)/shard_map/ppermute | solution.py:277
  75.8 8.1 %collective-permute-start.12 = (f32[296,128]{1,0:T(8,128)}, f32[296,128]{1,0:T(8,128)S(1)}, u32[]{:S(2)}, u32[]{:S(2)}) collective-permute-start(f32[296,128]{1,0:T(8,128)} %get-tuple-element.26), channel_id=1, source_target_pairs={{24,0},{25,1},{26,2},{27,3},{28,4},{29,5},{30,6},{31,7},{0,8},{1,9... | collective-permute-start | bytes 454664 | tf_op jit(solution)/shard_map/ppermute | solution.py:297
  78.1 9.9 %collective-permute-start.10 = (f32[296,128]{1,0:T(8,128)}, f32[296,128]{1,0:T(8,128)S(1)}, u32[]{:S(2)}, u32[]{:S(2)}) collective-permute-start(f32[296,128]{1,0:T(8,128)} %get-tuple-element.26), channel_id=1, source_target_pairs={{16,0},{17,1},{18,2},{19,3},{20,4},{21,5},{22,6},{23,7},{24,8},{25... | collective-permute-start | bytes 454664 | tf_op jit(solution)/shard_map/ppermute | solution.py:297
  80.9 8.3 %collective-permute-start.8 = (f32[296,128]{1,0:T(8,128)}, f32[296,128]{1,0:T(8,128)S(1)}, u32[]{:S(2)}, u32[]{:S(2)}) collective-permute-start(f32[296,128]{1,0:T(8,128)} %get-tuple-element.26), channel_id=1, source_target_pairs={{8,0},{9,1},{10,2},{11,3},{12,4},{13,5},{14,6},{15,7},{16,8},{17,9... | collective-permute-start | bytes 454664 | tf_op jit(solution)/shard_map/ppermute | solution.py:297
  84.0 6.7 %copy-start.8 = (f32[296,128]{1,0:T(8,128)}, f32[296,128]{1,0:T(8,128)S(1)}, u32[]{:S(2)}) copy-start(f32[296,128]{1,0:T(8,128)S(1)} %collective-permute-done.12.refs_4_) | copy-start | bytes 454660
  84.0 5.4 %collective-permute-start.13 = (f32[296,128]{1,0:T(8,128)S(1)}, f32[296,128]{1,0:T(8,128)S(1)}, u32[]{:S(2)}, u32[]{:S(2)}) collective-permute-start(f32[296,128]{1,0:T(8,128)S(1)} %collective-permute-done.12.refs_4_), channel_id=1, source_target_pairs={{0,1},{1,0},{2,3},{3,2},{4,5},{5,4},{6,7},{7,6},{8,9},{9,8},{10,11... | collective-permute-start | bytes 454664 | tf_op jit(solution)/shard_map/ppermute | solution.py:277
  88.1 2.5 %copy-start.10 = (f32[296,128]{1,0:T(8,128)}, f32[296,128]{1,0:T(8,128)S(1)}, u32[]{:S(2)}) copy-start(f32[296,128]{1,0:T(8,128)S(1)} %collective-permute-done.10.refs_2_) | copy-start | bytes 454660
  88.1 2.2 %collective-permute-start.11 = (f32[296,128]{1,0:T(8,128)S(1)}, f32[296,128]{1,0:T(8,128)S(1)}, u32[]{:S(2)}, u32[]{:S(2)}) collective-permute-start(f32[296,128]{1,0:T(8,128)S(1)} %collective-permute-done.10.refs_2_), channel_id=1, source_target_pairs={{0,1},{1,0},{2,3},{3,2},{4,5},{5,4},{6,7},{7,6},{8,9},{9,8},{10,11... | collective-permute-start | bytes 454664 | tf_op jit(solution)/shard_map/ppermute | solution.py:277
  89.2 1.4 %collective-permute-start.9 = (f32[296,128]{1,0:T(8,128)S(1)}, f32[296,128]{1,0:T(8,128)S(1)}, u32[]{:S(2)}, u32[]{:S(2)}) collective-permute-start(f32[296,128]{1,0:T(8,128)S(1)} %collective-permute-done.8.refs_0_), channel_id=1, source_target_pairs={{0,1},{1,0},{2,3},{3,2},{4,5},{5,4},{6,7},{7,6},{8,9},{9,8},{10,11... | collective-permute-start | bytes 454664 | tf_op jit(solution)/shard_map/ppermute | solution.py:277
  96.0 12.8 %collective-permute-start.18 = (f32[296,128]{1,0:T(8,128)}, f32[296,128]{1,0:T(8,128)S(1)}, u32[]{:S(2)}, u32[]{:S(2)}) collective-permute-start(f32[296,128]{1,0:T(8,128)} %get-tuple-element.30), channel_id=1, source_target_pairs={{96,0},{97,1},{98,2},{99,3},{100,4},{101,5},{102,6},{103,7},{104,8... | collective-permute-start | bytes 454664 | tf_op jit(solution)/shard_map/ppermute | solution.py:297
  97.3 12.4 %collective-permute-start.16 = (f32[296,128]{1,0:T(8,128)}, f32[296,128]{1,0:T(8,128)S(1)}, u32[]{:S(2)}, u32[]{:S(2)}) collective-permute-start(f32[296,128]{1,0:T(8,128)} %get-tuple-element.30), channel_id=1, source_target_pairs={{64,0},{65,1},{66,2},{67,3},{68,4},{69,5},{70,6},{71,7},{72,8},{73... | collective-permute-start | bytes 454664 | tf_op jit(solution)/shard_map/ppermute | solution.py:297
  98.6 11.2 %collective-permute-start.14 = (f32[296,128]{1,0:T(8,128)}, f32[296,128]{1,0:T(8,128)S(1)}, u32[]{:S(2)}, u32[]{:S(2)}) collective-permute-start(f32[296,128]{1,0:T(8,128)} %get-tuple-element.30), channel_id=1, source_target_pairs={{32,0},{33,1},{34,2},{35,3},{36,4},{37,5},{38,6},{39,7},{40,8},{41... | collective-permute-start | bytes 454664 | tf_op jit(solution)/shard_map/ppermute | solution.py:297
  108.8 2.5 %copy-start.1 = (f32[296,128]{1,0:T(8,128)}, f32[296,128]{1,0:T(8,128)S(1)}, u32[]{:S(2)}) copy-start(f32[296,128]{1,0:T(8,128)S(1)} %collective-permute-done.18.refs_4_) | copy-start | bytes 454660
  108.8 1.9 %collective-permute-start.19 = (f32[296,128]{1,0:T(8,128)S(1)}, f32[296,128]{1,0:T(8,128)S(1)}, u32[]{:S(2)}, u32[]{:S(2)}) collective-permute-start(f32[296,128]{1,0:T(8,128)S(1)} %collective-permute-done.18.refs_4_), channel_id=1, source_target_pairs={{0,1},{1,0},{2,3},{3,2},{4,5},{5,4},{6,7},{7,6},{8,9},{9,8},{10,11... | collective-permute-start | bytes 454664 | tf_op jit(solution)/shard_map/ppermute | solution.py:277
  109.7 1.4 %collective-permute-start.17 = (f32[296,128]{1,0:T(8,128)S(1)}, f32[296,128]{1,0:T(8,128)S(1)}, u32[]{:S(2)}, u32[]{:S(2)}) collective-permute-start(f32[296,128]{1,0:T(8,128)S(1)} %collective-permute-done.16.refs_2_), channel_id=1, source_target_pairs={{0,1},{1,0},{2,3},{3,2},{4,5},{5,4},{6,7},{7,6},{8,9},{9,8},{10,11... | collective-permute-start | bytes 454664 | tf_op jit(solution)/shard_map/ppermute | solution.py:277
  109.8 1.5 %collective-permute-start.15 = (f32[296,128]{1,0:T(8,128)S(1)}, f32[296,128]{1,0:T(8,128)S(1)}, u32[]{:S(2)}, u32[]{:S(2)}) collective-permute-start(f32[296,128]{1,0:T(8,128)S(1)} %collective-permute-done.14.refs_0_), channel_id=1, source_target_pairs={{0,1},{1,0},{2,3},{3,2},{4,5},{5,4},{6,7},{7,6},{8,9},{9,8},{10,11... | collective-permute-start | bytes 454664 | tf_op jit(solution)/shard_map/ppermute | solution.py:277
  (16 other events, 16.7 us)

commit v3 on v2

--- a/solution.py
+++ b/solution.py
@@ -11,7 +11,7 @@
 F32 = jnp.float32
 W = 192
 STEPS = 8
-ROWS = 592
+ROWS = 528
 HALF = ROWS // 2
 VMEM_LIMIT = 60 << 20
 
@@ -48,17 +48,18 @@
 def packed(e, l, u, ref):
     ref[0:192, :] = e[:, :128]
     ref[192:384, :] = jnp.concatenate([e[:, 128:], l[:, 128:]], 1)
-    ref[384:576, :] = l[:, :128]
-    ref[576:592, :] = jnp.zeros((16, 128), F32)
-    ref[576:577, :] = u[0:1, :128]
-    ref[577:578, 0:64] = u[0:1, 128:]
+    ref[384:512, :] = l[:128, :128]
+    ref[512:528, :] = jnp.zeros((16, 128), F32)
+    ref[512:513, :] = u[0:1, :128]
+    ref[513:514, 0:64] = u[0:1, 128:]
 
 
 def unpacked(ref):
     tail = ref[192:384, :]
     e = jnp.concatenate([ref[0:192, :], tail[:, :64]], 1)
-    l = jnp.concatenate([ref[384:576, :], tail[:, 64:]], 1)
-    u = jnp.concatenate([ref[576:577, :], ref[577:578, 0:64]], 1)
+    side = tail[:, 64:]
+    l = jnp.concatenate([jnp.concatenate([ref[384:512, :], side[:128].T], 0), side], 1)
+    u = jnp.concatenate([ref[512:513, :], ref[513:514, 0:64]], 1)
     return e, l, jnp.broadcast_to(u, (16, W))
 
 

time: 126 us -> 124 us (0.984)
  waiting for transfers between devices: 25 us -> 22.8 us
    ppermute x9, waiting for transfers between devices: 20.4 us -> 18.3 us  [gathered(): mine = lax.ppermute(half, 'tm', pairs)]
  transfers between devices with their start and end apart: 20 -> 20, of which waited for: 13 -> 13; matrix products, arithmetic and copies ran while one was open for 1% -> 0% of each run, Pallas kernels for 8% -> 9%
where the time goes in v3:
time: 124 us
  Pallas kernels  71 us (57%)
  starting transfers between devices  24.3 us (20%)
  waiting for transfers between devices  22.8 us (18%)
  local copies, waits for them, and re-layouts  4.29 us (3%)
    pallas_call x1, Pallas kernels, on_device(): pl.pallas_call(fold_kernel, grid=(blocks,), in_specs=[once, down, down3,...  34.4 us
    ppermute x9, waiting for transfers between devices, gathered(): mine = lax.ppermute(half, 'tm', pairs)  18.3 us
    ppermute x9, starting transfers between devices, gathered(): mine = lax.ppermute(half, 'tm', pairs)  15.5 us
    pallas_call x1, Pallas kernels, on_device(): pl.pallas_call(finish_kernel, grid=(blocks,), in_specs=[SCALAR] + [flat]...  14.1 us
    pallas_call x1, Pallas kernels, on_device(): pl.pallas_call(cross_kernel, grid=(blocks,), in_specs=[vec, mat, mat], ou...  10.6 us
    pallas_call x2, Pallas kernels, on_device(): pl.pallas_call(functools.partial(quad_kernel, level), in_specs=[SCALAR] +...  9.3 us
    ppermute x10, starting transfers between devices, other_core(): return lax.ppermute(part, 'tm', [(i, i ^ 1) for i in range(peers)])  5.48 us
    ppermute x10, waiting for transfers between devices, other_core(): return lax.ppermute(part, 'tm', [(i, i ^ 1) for i in range(peers)])  4.48 us
  transfers between devices with their start and end apart: 20, of which 13 were waited for; matrix products, arithmetic and copies ran while one was open for 0% of the time, Pallas kernels for 9%

profile of v3, /device:TPU:1, one launch (start us, length us, event | category | flops | bytes accessed | tf_op | source)
XLA Modules:
  0.0 123.8 jit_solution(12215923741501324918)
XLA Ops:
  0.6 0.9 slice.3
  1.6 3.3 %collective-permute-start = (f32[1,192,192]{2,1,0:T(8,128)S(1)}, f32[1,192,192]{2,1,0:T(8,128)S(1)}, u32[]{:S(2)}, u32[]{:S(2)}) collective-permute-start(f32[1,192,192]{2,1,0:T(8,128)S(1)} %slice.3), channel_id=1, source_target_pairs={{1,0},{2,1},{3,2},{4,3},{5,4},{6,5},{7,6},{8,7},{9,8},{10,9},{11,1... | collective-permute-start | bytes 442376 | tf_op jit(solution)/shard_map/ppermute | solution.py:235
  4.9 10.6 %cross.1 = (f32[32,192,192]{2,1,0:T(8,128)}, f32[32,192]{1,0:T(8,128)}) custom-call(f32[32,192]{1,0:T(8,128)} %mean.3, f32[32,192,192]{2,1,0:T(8,128)} %cov.3, f32[32,192,192]{2,1,0:T(8,128)} %dyn.1), custom_call_target="tpu_custom_call" | custom-call | flops 2717908992 | bytes 18874368 | tf_op jit(solution)/shard_map/cross/pallas_call | solution.py:242
  16.2 34.4 %fold.1 = (f32[32,192,192]{2,1,0:T(8,128)}, f32[32,192,192]{2,1,0:T(8,128)}, f32[32,192]{1,0:T(8,128)}, f32[528,128]{1,0:T(8,128)}) custom-call(f32[1,192,192]{2,1,0:T(8,128)} %copy-done.7, f32[32,192]{1,0:T(8,128)} %mean.3, f32[32,192,192]{2,1,0:T(8,128)} %cov.3, f32[32,192,192]{2,1,0:T(8,128)} %get-tuple-element.18.cross, ...), custom_call_target="tpu_custom_call" | custom-call | flops 13589544960 | bytes 31457280 | tf_op jit(solution)/shard_map/fold/pallas_call | solution.py:256
  51.2 1.1 collective-permute-done.1.other
  53.1 2.6 %pair.1 = (f32[528,128]{1,0:T(8,128)}, f32[264,128]{1,0:T(8,128)}, f32[528,128]{1,0:T(8,128)}) custom-call(s32[4]{0:T(128)} %pad_add_fusion.place, f32[528,128]{1,0:T(8,128)} %get-tuple-element.20.own, f32[528,128]{1,0:T(8,128)} %copy-done), custom_call_target="tpu_custom_call" | custom-call | flops 127401984 | bytes 1081344 | tf_op jit(solution)/shard_map/pair/pallas_call | solution.py:280
  55.7 1.7 %collective-permute-start.6 = (f32[264,128]{1,0:T(8,128)}, f32[264,128]{1,0:T(8,128)S(1)}, u32[]{:S(2)}, u32[]{:S(2)}) collective-permute-start(f32[264,128]{1,0:T(8,128)} %get-tuple-element.23), channel_id=1, source_target_pairs={{6,0},{7,1},{0,2},{1,3},{2,4},{3,5},{4,6},{5,7},{14,8},{15,9},{8,1... | collective-permute-start | bytes 405512 | tf_op jit(solution)/shard_map/ppermute | solution.py:298
  57.4 3.3 %collective-permute-start.4 = (f32[264,128]{1,0:T(8,128)}, f32[264,128]{1,0:T(8,128)S(1)}, u32[]{:S(2)}, u32[]{:S(2)}) collective-permute-start(f32[264,128]{1,0:T(8,128)} %get-tuple-element.23), channel_id=1, source_target_pairs={{4,0},{5,1},{6,2},{7,3},{0,4},{1,5},{2,6},{3,7},{12,8},{13,9},{14,... | collective-permute-start | bytes 405512 | tf_op jit(solution)/shard_map/ppermute | solution.py:298
  61.5 2.1 %collective-permute-done.6.refs_4_ = f32[264,128]{1,0:T(8,128)S(1)} collective-permute-done((f32[264,128]{1,0:T(8,128)}, f32[264,128]{1,0:T(8,128)S(1)}, u32[]{:S(2)}, u32[]{:S(2)}) %collective-permute-start.6) | collective-permute-done | bytes 135200 | tf_op jit(solution)/shard_map/ppermute | solution.py:298
  64.3 3.1 %collective-permute-done.4.refs_2_ = f32[264,128]{1,0:T(8,128)S(1)} collective-permute-done((f32[264,128]{1,0:T(8,128)}, f32[264,128]{1,0:T(8,128)S(1)}, u32[]{:S(2)}, u32[]{:S(2)}) %collective-permute-start.4) | collective-permute-done | bytes 135200 | tf_op jit(solution)/shard_map/ppermute | solution.py:298
  67.4 0.9 collective-permute-start.5
  70.4 4.6 %quad.2 = (f32[528,128]{1,0:T(8,128)}, f32[264,128]{1,0:T(8,128)}, f32[528,128]{1,0:T(8,128)}, f32[528,128]{1,0:T(8,128)}) custom-call(s32[4]{0:T(128)} %pad_add_fusion.place, f32[528,128]{1,0:T(8,128)} %get-tuple-element.21.near.follow, f32[528,128]{1,0:T(8,128)} %get-tuple-element.21.near.follow, f32[528,128]{1,0:T(8,128)} %get-tuple-element.22.own, ...), custom_call_target="tpu_custom_call" | custom-call | flops 637009920 | bytes 2703360 | tf_op jit(solution)/shard_map/quad/pallas_call | solution.py:305
  75.0 2.3 %collective-permute-start.12 = (f32[264,128]{1,0:T(8,128)}, f32[264,128]{1,0:T(8,128)S(1)}, u32[]{:S(2)}, u32[]{:S(2)}) collective-permute-start(f32[264,128]{1,0:T(8,128)} %get-tuple-element.26), channel_id=1, source_target_pairs={{24,0},{25,1},{26,2},{27,3},{28,4},{29,5},{30,6},{31,7},{0,8},{1,9... | collective-permute-start | bytes 405512 | tf_op jit(solution)/shard_map/ppermute | solution.py:298
  77.3 2.7 %collective-permute-start.10 = (f32[264,128]{1,0:T(8,128)}, f32[264,128]{1,0:T(8,128)S(1)}, u32[]{:S(2)}, u32[]{:S(2)}) collective-permute-start(f32[264,128]{1,0:T(8,128)} %get-tuple-element.26), channel_id=1, source_target_pairs={{16,0},{17,1},{18,2},{19,3},{20,4},{21,5},{22,6},{23,7},{24,8},{25... | collective-permute-start | bytes 405512 | tf_op jit(solution)/shard_map/ppermute | solution.py:298
  80.9 1.9 %collective-permute-done.12.refs_4_ = f32[264,128]{1,0:T(8,128)S(1)} collective-permute-done((f32[264,128]{1,0:T(8,128)}, f32[264,128]{1,0:T(8,128)S(1)}, u32[]{:S(2)}, u32[]{:S(2)}) %collective-permute-start.12) | collective-permute-done | bytes 135200 | tf_op jit(solution)/shard_map/ppermute | solution.py:298
  83.6 2.9 %collective-permute-done.10.refs_2_ = f32[264,128]{1,0:T(8,128)S(1)} collective-permute-done((f32[264,128]{1,0:T(8,128)}, f32[264,128]{1,0:T(8,128)S(1)}, u32[]{:S(2)}, u32[]{:S(2)}) %collective-permute-start.10) | collective-permute-done | bytes 135200 | tf_op jit(solution)/shard_map/ppermute | solution.py:298
  86.6 1.2 collective-permute-start.11
  87.8 0.9 collective-permute-done.11.refs_3_
  89.8 4.7 %quad.3 = (f32[528,128]{1,0:T(8,128)}, f32[264,128]{1,0:T(8,128)}, f32[528,128]{1,0:T(8,128)}, f32[528,128]{1,0:T(8,128)}) custom-call(s32[4]{0:T(128)} %pad_add_fusion.place, f32[528,128]{1,0:T(8,128)} %get-tuple-element.21.near.follow, f32[528,128]{1,0:T(8,128)} %get-tuple-element.24.follow, f32[528,128]{1,0:T(8,128)} %get-tuple-element.25.own, ...), custom_call_target="tpu_custom_call" | custom-call | flops 637009920 | bytes 2703360 | tf_op jit(solution)/shard_map/quad/pallas_call | solution.py:305
  94.4 1.3 %collective-permute-start.18 = (f32[264,128]{1,0:T(8,128)}, f32[264,128]{1,0:T(8,128)S(1)}, u32[]{:S(2)}, u32[]{:S(2)}) collective-permute-start(f32[264,128]{1,0:T(8,128)} %get-tuple-element.30), channel_id=1, source_target_pairs={{96,0},{97,1},{98,2},{99,3},{100,4},{101,5},{102,6},{103,7},{104,8... | collective-permute-start | bytes 405512 | tf_op jit(solution)/shard_map/ppermute | solution.py:298
  95.7 1.3 %collective-permute-start.16 = (f32[264,128]{1,0:T(8,128)}, f32[264,128]{1,0:T(8,128)S(1)}, u32[]{:S(2)}, u32[]{:S(2)}) collective-permute-start(f32[264,128]{1,0:T(8,128)} %get-tuple-element.30), channel_id=1, source_target_pairs={{64,0},{65,1},{66,2},{67,3},{68,4},{69,5},{70,6},{71,7},{72,8},{73... | collective-permute-start | bytes 405512 | tf_op jit(solution)/shard_map/ppermute | solution.py:298
  97.0 1.3 %collective-permute-start.14 = (f32[264,128]{1,0:T(8,128)}, f32[264,128]{1,0:T(8,128)S(1)}, u32[]{:S(2)}, u32[]{:S(2)}) collective-permute-start(f32[264,128]{1,0:T(8,128)} %get-tuple-element.30), channel_id=1, source_target_pairs={{32,0},{33,1},{34,2},{35,3},{36,4},{37,5},{38,6},{39,7},{40,8},{41... | collective-permute-start | bytes 405512 | tf_op jit(solution)/shard_map/ppermute | solution.py:298
  98.3 8.3 %collective-permute-done.18.refs_4_ = f32[264,128]{1,0:T(8,128)S(1)} collective-permute-done((f32[264,128]{1,0:T(8,128)}, f32[264,128]{1,0:T(8,128)S(1)}, u32[]{:S(2)}, u32[]{:S(2)}) %collective-permute-start.18) | collective-permute-done | bytes 135200 | tf_op jit(solution)/shard_map/ppermute | solution.py:298
  109.6 14.1 %finish.1 = (f32[32,192]{1,0:T(8,128)}, f32[32,192,192]{2,1,0:T(8,128)}) custom-call(s32[4]{0:T(128)} %pad_add_fusion.place, f32[528,128]{1,0:T(8,128)} %get-tuple-element.27.near, f32[528,128]{1,0:T(8,128)} %get-tuple-element.28.follow, f32[528,128]{1,0:T(8,128)} %get-tuple-element.29.own, f32[264,128]{1,0:T(8,128)} %copy-done.3, f32[264,128]{1,0:T(8,128)} %copy-done.6, ...), custom_call_target="tpu_custom_call" | custom-call | flops 2717908992 | bytes 18874368 | tf_op jit(solution)/shard_map/finish/pallas_call | solution.py:320
  (64 shorter events, 11.4 us)
Async XLA Ops:
  1.6 13.9 %collective-permute-start = (f32[1,192,192]{2,1,0:T(8,128)S(1)}, f32[1,192,192]{2,1,0:T(8,128)S(1)}, u32[]{:S(2)}, u32[]{:S(2)}) collective-permute-start(f32[1,192,192]{2,1,0:T(8,128)S(1)} %slice.3), channel_id=1, source_target_pairs={{1,0},{2,1},{3,2},{4,3},{5,4},{6,5},{7,6},{8,7},{9,8},{10,9},{11,1... | collective-permute-start | bytes 442376 | tf_op jit(solution)/shard_map/ppermute | solution.py:235
  50.5 1.8 %collective-permute-start.1 = (f32[528,128]{1,0:T(8,128)}, f32[528,128]{1,0:T(8,128)S(1)}, u32[]{:S(2)}, u32[]{:S(2)}) collective-permute-start(f32[528,128]{1,0:T(8,128)} %get-tuple-element.20.own), channel_id=1, source_target_pairs={{0,1},{1,0},{2,3},{3,2},{4,5},{5,4},{6,7},{7,6},{8,9},{9,8},{10,11... | collective-permute-start | bytes 811016 | tf_op jit(solution)/shard_map/ppermute | solution.py:278
  55.7 7.9 %collective-permute-start.6 = (f32[264,128]{1,0:T(8,128)}, f32[264,128]{1,0:T(8,128)S(1)}, u32[]{:S(2)}, u32[]{:S(2)}) collective-permute-start(f32[264,128]{1,0:T(8,128)} %get-tuple-element.23), channel_id=1, source_target_pairs={{6,0},{7,1},{0,2},{1,3},{2,4},{3,5},{4,6},{5,7},{14,8},{15,9},{8,1... | collective-permute-start | bytes 405512 | tf_op jit(solution)/shard_map/ppermute | solution.py:298
  57.4 10.0 %collective-permute-start.4 = (f32[264,128]{1,0:T(8,128)}, f32[264,128]{1,0:T(8,128)S(1)}, u32[]{:S(2)}, u32[]{:S(2)}) collective-permute-start(f32[264,128]{1,0:T(8,128)} %get-tuple-element.23), channel_id=1, source_target_pairs={{4,0},{5,1},{6,2},{7,3},{0,4},{1,5},{2,6},{3,7},{12,8},{13,9},{14,... | collective-permute-start | bytes 405512 | tf_op jit(solution)/shard_map/ppermute | solution.py:298
  60.7 7.6 %collective-permute-start.2 = (f32[264,128]{1,0:T(8,128)}, f32[264,128]{1,0:T(8,128)S(1)}, u32[]{:S(2)}, u32[]{:S(2)}) collective-permute-start(f32[264,128]{1,0:T(8,128)} %get-tuple-element.23), channel_id=1, source_target_pairs={{2,0},{3,1},{4,2},{5,3},{6,4},{7,5},{0,6},{1,7},{10,8},{11,9},{12,... | collective-permute-start | bytes 405512 | tf_op jit(solution)/shard_map/ppermute | solution.py:298
  63.6 6.2 %copy-start.9 = (f32[264,128]{1,0:T(8,128)}, f32[264,128]{1,0:T(8,128)S(1)}, u32[]{:S(2)}) copy-start(f32[264,128]{1,0:T(8,128)S(1)} %collective-permute-done.6.refs_4_) | copy-start | bytes 405508
  63.6 5.1 %collective-permute-start.7 = (f32[264,128]{1,0:T(8,128)S(1)}, f32[264,128]{1,0:T(8,128)S(1)}, u32[]{:S(2)}, u32[]{:S(2)}) collective-permute-start(f32[264,128]{1,0:T(8,128)S(1)} %collective-permute-done.6.refs_4_), channel_id=1, source_target_pairs={{0,1},{1,0},{2,3},{3,2},{4,5},{5,4},{6,7},{7,6},{8,9},{9,8},{10,11... | collective-permute-start | bytes 405512 | tf_op jit(solution)/shard_map/ppermute | solution.py:278
  67.4 1.9 %collective-permute-start.5 = (f32[264,128]{1,0:T(8,128)S(1)}, f32[264,128]{1,0:T(8,128)S(1)}, u32[]{:S(2)}, u32[]{:S(2)}) collective-permute-start(f32[264,128]{1,0:T(8,128)S(1)} %collective-permute-done.4.refs_2_), channel_id=1, source_target_pairs={{0,1},{1,0},{2,3},{3,2},{4,5},{5,4},{6,7},{7,6},{8,9},{9,8},{10,11... | collective-permute-start | bytes 405512 | tf_op jit(solution)/shard_map/ppermute | solution.py:278
  68.4 1.4 %collective-permute-start.3 = (f32[264,128]{1,0:T(8,128)S(1)}, f32[264,128]{1,0:T(8,128)S(1)}, u32[]{:S(2)}, u32[]{:S(2)}) collective-permute-start(f32[264,128]{1,0:T(8,128)S(1)} %collective-permute-done.2.refs_0_), channel_id=1, source_target_pairs={{0,1},{1,0},{2,3},{3,2},{4,5},{5,4},{6,7},{7,6},{8,9},{9,8},{10,11... | collective-permute-start | bytes 405512 | tf_op jit(solution)/shard_map/ppermute | solution.py:278
  75.0 7.8 %collective-permute-start.12 = (f32[264,128]{1,0:T(8,128)}, f32[264,128]{1,0:T(8,128)S(1)}, u32[]{:S(2)}, u32[]{:S(2)}) collective-permute-start(f32[264,128]{1,0:T(8,128)} %get-tuple-element.26), channel_id=1, source_target_pairs={{24,0},{25,1},{26,2},{27,3},{28,4},{29,5},{30,6},{31,7},{0,8},{1,9... | collective-permute-start | bytes 405512 | tf_op jit(solution)/shard_map/ppermute | solution.py:298
  77.3 9.2 %collective-permute-start.10 = (f32[264,128]{1,0:T(8,128)}, f32[264,128]{1,0:T(8,128)S(1)}, u32[]{:S(2)}, u32[]{:S(2)}) collective-permute-start(f32[264,128]{1,0:T(8,128)} %get-tuple-element.26), channel_id=1, source_target_pairs={{16,0},{17,1},{18,2},{19,3},{20,4},{21,5},{22,6},{23,7},{24,8},{25... | collective-permute-start | bytes 405512 | tf_op jit(solution)/shard_map/ppermute | solution.py:298
  80.1 7.6 %collective-permute-start.8 = (f32[264,128]{1,0:T(8,128)}, f32[264,128]{1,0:T(8,128)S(1)}, u32[]{:S(2)}, u32[]{:S(2)}) collective-permute-start(f32[264,128]{1,0:T(8,128)} %get-tuple-element.26), channel_id=1, source_target_pairs={{8,0},{9,1},{10,2},{11,3},{12,4},{13,5},{14,6},{15,7},{16,8},{17,9... | collective-permute-start | bytes 405512 | tf_op jit(solution)/shard_map/ppermute | solution.py:298
  82.8 6.3 %copy-start.8 = (f32[264,128]{1,0:T(8,128)}, f32[264,128]{1,0:T(8,128)S(1)}, u32[]{:S(2)}) copy-start(f32[264,128]{1,0:T(8,128)S(1)} %collective-permute-done.12.refs_4_) | copy-start | bytes 405508
  82.8 5.0 %collective-permute-start.13 = (f32[264,128]{1,0:T(8,128)S(1)}, f32[264,128]{1,0:T(8,128)S(1)}, u32[]{:S(2)}, u32[]{:S(2)}) collective-permute-start(f32[264,128]{1,0:T(8,128)S(1)} %collective-permute-done.12.refs_4_), channel_id=1, source_target_pairs={{0,1},{1,0},{2,3},{3,2},{4,5},{5,4},{6,7},{7,6},{8,9},{9,8},{10,11... | collective-permute-start | bytes 405512 | tf_op jit(solution)/shard_map/ppermute | solution.py:278
  86.6 2.5 %copy-start.10 = (f32[264,128]{1,0:T(8,128)}, f32[264,128]{1,0:T(8,128)S(1)}, u32[]{:S(2)}) copy-start(f32[264,128]{1,0:T(8,128)S(1)} %collective-permute-done.10.refs_2_) | copy-start | bytes 405508
  86.6 2.1 %collective-permute-start.11 = (f32[264,128]{1,0:T(8,128)S(1)}, f32[264,128]{1,0:T(8,128)S(1)}, u32[]{:S(2)}, u32[]{:S(2)}) collective-permute-start(f32[264,128]{1,0:T(8,128)S(1)} %collective-permute-done.10.refs_2_), channel_id=1, source_target_pairs={{0,1},{1,0},{2,3},{3,2},{4,5},{5,4},{6,7},{7,6},{8,9},{9,8},{10,11... | collective-permute-start | bytes 405512 | tf_op jit(solution)/shard_map/ppermute | solution.py:278
  87.7 1.4 %collective-permute-start.9 = (f32[264,128]{1,0:T(8,128)S(1)}, f32[264,128]{1,0:T(8,128)S(1)}, u32[]{:S(2)}, u32[]{:S(2)}) collective-permute-start(f32[264,128]{1,0:T(8,128)S(1)} %collective-permute-done.8.refs_0_), channel_id=1, source_target_pairs={{0,1},{1,0},{2,3},{3,2},{4,5},{5,4},{6,7},{7,6},{8,9},{9,8},{10,11... | collective-permute-start | bytes 405512 | tf_op jit(solution)/shard_map/ppermute | solution.py:278
  94.4 12.1 %collective-permute-start.18 = (f32[264,128]{1,0:T(8,128)}, f32[264,128]{1,0:T(8,128)S(1)}, u32[]{:S(2)}, u32[]{:S(2)}) collective-permute-start(f32[264,128]{1,0:T(8,128)} %get-tuple-element.30), channel_id=1, source_target_pairs={{96,0},{97,1},{98,2},{99,3},{100,4},{101,5},{102,6},{103,7},{104,8... | collective-permute-start | bytes 405512 | tf_op jit(solution)/shard_map/ppermute | solution.py:298
  95.7 11.7 %collective-permute-start.16 = (f32[264,128]{1,0:T(8,128)}, f32[264,128]{1,0:T(8,128)S(1)}, u32[]{:S(2)}, u32[]{:S(2)}) collective-permute-start(f32[264,128]{1,0:T(8,128)} %get-tuple-element.30), channel_id=1, source_target_pairs={{64,0},{65,1},{66,2},{67,3},{68,4},{69,5},{70,6},{71,7},{72,8},{73... | collective-permute-start | bytes 405512 | tf_op jit(solution)/shard_map/ppermute | solution.py:298
  97.0 10.5 %collective-permute-start.14 = (f32[264,128]{1,0:T(8,128)}, f32[264,128]{1,0:T(8,128)S(1)}, u32[]{:S(2)}, u32[]{:S(2)}) collective-permute-start(f32[264,128]{1,0:T(8,128)} %get-tuple-element.30), channel_id=1, source_target_pairs={{32,0},{33,1},{34,2},{35,3},{36,4},{37,5},{38,6},{39,7},{40,8},{41... | collective-permute-start | bytes 405512 | tf_op jit(solution)/shard_map/ppermute | solution.py:298
  106.6 2.4 %copy-start.1 = (f32[264,128]{1,0:T(8,128)}, f32[264,128]{1,0:T(8,128)S(1)}, u32[]{:S(2)}) copy-start(f32[264,128]{1,0:T(8,128)S(1)} %collective-permute-done.18.refs_4_) | copy-start | bytes 405508
  106.6 1.9 %collective-permute-start.19 = (f32[264,128]{1,0:T(8,128)S(1)}, f32[264,128]{1,0:T(8,128)S(1)}, u32[]{:S(2)}, u32[]{:S(2)}) collective-permute-start(f32[264,128]{1,0:T(8,128)S(1)} %collective-permute-done.18.refs_4_), channel_id=1, source_target_pairs={{0,1},{1,0},{2,3},{3,2},{4,5},{5,4},{6,7},{7,6},{8,9},{9,8},{10,11... | collective-permute-start | bytes 405512 | tf_op jit(solution)/shard_map/ppermute | solution.py:278
  107.4 1.4 %collective-permute-start.17 = (f32[264,128]{1,0:T(8,128)S(1)}, f32[264,128]{1,0:T(8,128)S(1)}, u32[]{:S(2)}, u32[]{:S(2)}) collective-permute-start(f32[264,128]{1,0:T(8,128)S(1)} %collective-permute-done.16.refs_2_), channel_id=1, source_target_pairs={{0,1},{1,0},{2,3},{3,2},{4,5},{5,4},{6,7},{7,6},{8,9},{9,8},{10,11... | collective-permute-start | bytes 405512 | tf_op jit(solution)/shard_map/ppermute | solution.py:278
  107.5 1.4 %collective-permute-start.15 = (f32[264,128]{1,0:T(8,128)S(1)}, f32[264,128]{1,0:T(8,128)S(1)}, u32[]{:S(2)}, u32[]{:S(2)}) collective-permute-start(f32[264,128]{1,0:T(8,128)S(1)} %collective-permute-done.14.refs_0_), channel_id=1, source_target_pairs={{0,1},{1,0},{2,3},{3,2},{4,5},{5,4},{6,7},{7,6},{8,9},{9,8},{10,11... | collective-permute-start | bytes 405512 | tf_op jit(solution)/shard_map/ppermute | solution.py:278
  (16 other events, 16.5 us)
